TPU v7x, 512 devices: a whole 4x4x16 slice. The times are simulated.
512 devices in a mesh: dp: 4 (over x), ctx: 128 (over y, z, core).
Axes of the slice: x: 4, y: 4, z: 16, core: 2. Of those that a mesh axis runs over, the one named last changes fastest.
Arguments:
- queries: bfloat16 [4, 16384, 8192], P('dp', 'ctx'), may hold values from -80 to 80
- grad_out: bfloat16 [4, 16384, 8192], P('dp', 'ctx'), may hold values from -6 to 6
- seq_lse: float32 [4, 16384, 64], P('dp', 'ctx'), may hold values from 4 to 10
- out_dot: float32 [4, 16384, 64], P('dp', 'ctx'), may hold values from -24 to 24
- prefix: bfloat16 [256, 2, 512], replicated, may hold values from -12 to 12
Outputs:
- updated: float32 [256, 2, 512], P('ctx')
All inputs are finite; a program needn't handle non-finite values.
Results may differ from a plain program's by a relative error of at most 0.0013.
Values sent between devices are 32-bit elements; how exact they have to be, the bound alone decides.
No kernel may reach another device: no remote copies, remote signals or barrier semaphores. Data moves between devices by JAX's collectives and lax.ppermute only.
A program may use at most 64 MiB of HBM per device.

v0:
```python
import jax
import jax.numpy as jnp
from jax import lax
from jax.sharding import PartitionSpec as P

HEAD = 128


def body(queries, grad_out, seq_lse, out_dot, prefix):
    kv_count = prefix.shape[2] // HEAD
    tok_rows = queries.shape[1]
    groups = queries.shape[2] // (kv_count * HEAD)
    rows_all = prefix.shape[0]
    scale = HEAD ** (-0.5)
    q_local = queries.reshape(tok_rows, kv_count, groups, HEAD)
    d_local = grad_out.reshape(tok_rows, kv_count, groups, HEAD)
    lse_local = seq_lse.reshape(tok_rows, kv_count, groups)
    delta = out_dot.reshape(tok_rows, kv_count, groups)
    keys = prefix[:, 0, :].reshape(rows_all, kv_count, HEAD)
    values = prefix[:, 1, :].reshape(rows_all, kv_count, HEAD)
    scores = scale * jnp.einsum("rgjd,pgd->rgjp", q_local, keys, preferred_element_type=jnp.float32)
    top = jnp.max(scores, axis=-1)
    prefix_lse = top + jnp.log(jnp.sum(jnp.exp(scores - top[..., None]), axis=-1))
    total = jnp.logaddexp(lse_local, prefix_lse)
    own_rows = rows_all // lax.axis_size("ctx")
    first_row = lax.axis_index("ctx") * own_rows
    probs = jnp.exp(scores - total[..., None])
    probs_low = probs.astype(jnp.bfloat16)
    grad_v = jnp.einsum("rgjp,rgjd->pgd", probs_low, d_local, preferred_element_type=jnp.float32)
    dprobs = jnp.einsum("rgjd,pgd->rgjp", d_local, values, preferred_element_type=jnp.float32)
    dscores = (probs * (dprobs - delta[..., None])).astype(jnp.bfloat16)
    grad_k = scale * jnp.einsum(
        "rgjp,rgjd->pgd", dscores, q_local, preferred_element_type=jnp.float32
    )
    grads = lax.psum(
        jnp.stack(
            [grad_k.reshape(rows_all, kv_count * HEAD), grad_v.reshape(rows_all, kv_count * HEAD)],
            1,
        ),
        ("dp", "ctx"),
    )
    grad_ms = jnp.mean(grads * grads, axis=(0, 2))
    own_grads = lax.dynamic_slice_in_dim(grads, first_row, own_rows, 0)
    weights = prefix.astype(jnp.float32)
    weight_ms = jnp.mean(weights * weights, axis=(0, 2))
    ratio = jnp.sqrt(weight_ms) / jnp.sqrt(grad_ms + 1e-06)
    own_weights = lax.dynamic_slice_in_dim(weights, first_row, own_rows, 0)
    return own_weights - 0.5 * ratio[None, :, None] * own_grads


def solution(mesh):
    return jax.shard_map(
        body,
        mesh=mesh,
        in_specs=(
            P("dp", "ctx", None),
            P("dp", "ctx", None),
            P("dp", "ctx", None),
            P("dp", "ctx", None),
            P(),
        ),
        out_specs=P("ctx", None, None),
        check_vma=False,
    )
```

profile of v0, /device:TPU:1, one launch (start us, length us, event | category | flops | bytes accessed | tf_op | source)
XLA Modules:
  0.0 517.7 jit_solution(16994881866388246729)
XLA Ops:
  6.5 0.0 all-reduce.2.cloned.1.call-start
  6.5 3.2 copy.34
  9.8 2.2 fusion.22
  11.9 0.5 copy.32
  12.4 4.1 copy.31
  16.5 1.1 copy.33
  17.6 0.0 copy-start.4
  17.6 0.0 copy-start.2
  17.6 1.3 bitcast_reduce_fusion
  18.9 0.0 copy-start
  18.9 0.0 copy-start.3
  18.9 0.0 copy-start.5
  18.9 1.8 fusion.3
  20.8 0.0 copy-done.4
  20.8 0.0 copy-done.2
  20.8 1.9 fusion.6
  22.7 0.0 copy-done
  22.7 0.0 copy-done.3
  22.7 0.0 copy-done.5
  22.7 0.0 copy-start.1
  22.7 8.2 %fusion.17 = f32[4,256,128]{1,2,0:T(8,128)} fusion(bf16[128,4,16,128]{0,3,2,1:T(8,128)(2,1)S(1)} %bitcast.66, f32[4,256,128,16]{2,1,3,0:T(8,128)} %copy-done, f32[128,4,16]{0,2,1:T(8,128)S(1)} %bitcast.74, f32[128,4,16]{0,2,1:T(8,128)S(1)} %add_select_fusion, bf16[256,4,128,1]{0,2,3,1:T(8,128)(2,1)S(1)} %bitcast.72, bf16[128,4,16,128]{0,3,2,1:T(8,128)(2,1)} %bitcast.67), kind=kOutput, calls=%fused_computation.16 | convolution fusion | flops 1084358656 | bytes 13434880 | tf_op jit(solution)/shard_map/rgjp,rgjd->pgd/dot_general | solution.py:32
  30.9 1.3 copy.21
  32.2 0.6 copy.22
  32.8 2.0 pad_maximum_fusion
  34.8 0.0 all-reduce.2.cloned.1.call-update
  34.8 0.0 copy-done.1
  34.8 0.4 convert_element_type.9
  35.2 1.2 multiply_reduce_fusion.1
  36.4 470.7 %all-reduce.2.cloned.1.call-done = f32[256,2,512]{2,1,0:T(2,128)} async-done(((f32[256,2,512]{2,1,0:T(2,128)}), f32[256,2,512]{2,1,0:T(2,128)}) %all-reduce.2.cloned.1.call-update) | async-done | bytes 1048592 | tf_op jit(solution)/shard_map/psum | solution.py:35
  507.1 2.4 multiply_reduce_fusion
  509.5 1.4 multiply_subtract_fusion
  (2 shorter events, 0.1 us)
Async XLA Ops:
  6.5 500.6 %all-reduce.2.cloned.1.call-start = ((), (), s32[]{:S(2)}) async-start(), calls=%async_computation | async-start | bytes 2097152 | tf_op jit(solution)/shard_map/psum | solution.py:35
  17.6 3.2 copy-start.4
  17.6 3.2 copy-start.2
  18.9 3.8 copy-start
  18.9 3.8 copy-start.3
  18.9 3.8 copy-start.5
  22.7 12.0 %copy-start.1 = (bf16[256,2,512]{2,1,0:T(2,128)(2,1)S(1)}, bf16[256,2,512]{2,1,0:T(2,128)(2,1)}, u32[]{:S(2)}) copy-start(bf16[256,2,512]{2,1,0:T(2,128)(2,1)} %param.9) | copy-start | bytes 1572868
Sparse Core Ops, SparseCore 0:
  34.9 472.1 all-reduce.1
where the time goes:
time: 518 us
  waiting for transfers between devices  471 us (91%)
  between operations  13.6 us (3%)
  local copies, waits for them, and re-layouts  12.9 us (2%)
  matrix products  11.3 us (2%)
  other arithmetic  9.21 us (2%)
    psum x1, waiting for transfers between devices, body(): lax.psum(jnp.stack([grad_k.reshape(rows_all, kv_count * HEAD), grad_v.res...  471 us
  transfers between devices with their start and end apart: 1, of which 1 were waited for; matrix products, arithmetic and copies ran while one was open for 0% of the time, Pallas kernels for 0%

commit v1 on v0

v1 whole, which is shorter than its diff:
```python
import jax
import jax.numpy as jnp
from jax import lax
from jax.sharding import Mesh, PartitionSpec as P

HEAD = 128


def local_grads(queries, grad_out, seq_lse, out_dot, prefix):
    kv_count = prefix.shape[2] // HEAD
    tok_rows = queries.shape[1]
    groups = queries.shape[2] // (kv_count * HEAD)
    rows_all = prefix.shape[0]
    scale = HEAD ** (-0.5)
    q_local = queries.reshape(tok_rows, kv_count, groups, HEAD)
    d_local = grad_out.reshape(tok_rows, kv_count, groups, HEAD)
    lse_local = seq_lse.reshape(tok_rows, kv_count, groups)
    delta = out_dot.reshape(tok_rows, kv_count, groups)
    keys = prefix[:, 0, :].reshape(rows_all, kv_count, HEAD)
    values = prefix[:, 1, :].reshape(rows_all, kv_count, HEAD)
    scores = scale * jnp.einsum("rgjd,pgd->rgjp", q_local, keys, preferred_element_type=jnp.float32)
    top = jnp.max(scores, axis=-1)
    prefix_lse = top + jnp.log(jnp.sum(jnp.exp(scores - top[..., None]), axis=-1))
    total = jnp.logaddexp(lse_local, prefix_lse)
    probs = jnp.exp(scores - total[..., None])
    probs_low = probs.astype(jnp.bfloat16)
    grad_v = jnp.einsum("rgjp,rgjd->pgd", probs_low, d_local, preferred_element_type=jnp.float32)
    dprobs = jnp.einsum("rgjd,pgd->rgjp", d_local, values, preferred_element_type=jnp.float32)
    dscores = (probs * (dprobs - delta[..., None])).astype(jnp.bfloat16)
    grad_k = scale * jnp.einsum(
        "rgjp,rgjd->pgd", dscores, q_local, preferred_element_type=jnp.float32
    )
    return grad_k, grad_v


def make_body(nx, ny, nz, nc):
    def body(queries, grad_out, seq_lse, out_dot, prefix):
        rows_all, width = prefix.shape[0], prefix.shape[2]
        own = rows_all // (ny * nz * nc)
        part = width // nx
        grad_k, grad_v = local_grads(queries, grad_out, seq_lse, out_dot, prefix)
        grads = jnp.stack([grad_k, grad_v], 0).reshape(2, ny, nz, nc, own, nx, part)
        grads = grads.transpose(3, 5, 1, 2, 0, 4, 6)
        core = lax.axis_index("c")
        mine = lax.dynamic_index_in_dim(grads, core, 0, keepdims=False)
        other = lax.dynamic_index_in_dim(grads, 1 - core, 0, keepdims=False)
        pairs = [(i, (i + 1) % nc) for i in range(nc)]
        half = mine + lax.ppermute(other, "c", pairs)
        rows = nz * 2 * own
        plane = lax.all_to_all(
            half.reshape(nx * ny, rows, part), ("x", "y"), 0, 0, tiled=True
        ).sum(0)
        piece = lax.all_to_all(
            plane.reshape(nz, 2 * own, part), "z", 0, 0, tiled=True
        ).sum(0)
        squares = (piece * piece).reshape(2, own, part).sum(1)
        squares = lax.all_to_all(
            jnp.broadcast_to(squares[None], (nz, 2, part)), "z", 0, 0, tiled=True
        ).sum(0)
        packed = jnp.concatenate([piece, squares], 0)
        count = nx * ny * nc
        packed = lax.all_to_all(
            jnp.broadcast_to(packed[None], (count,) + packed.shape),
            ("x", "y", "c"), 0, 0, tiled=True,
        )
        grad_ms = packed[:, 2 * own:].sum((0, 2)) / (rows_all * width)
        packed = packed.reshape(nx, ny * nc, 2 * own + 2, part)
        place = lax.axis_index("y") * nc + core
        mean = lax.dynamic_index_in_dim(packed, place, 1, keepdims=False)[:, : 2 * own]
        own_grads = mean.reshape(nx, 2, own, part).transpose(2, 1, 0, 3).reshape(own, 2, width)
        weights = prefix.astype(jnp.float32)
        weight_ms = jnp.mean(weights * weights, axis=(0, 2))
        ratio = jnp.sqrt(weight_ms) / jnp.sqrt(grad_ms + 1e-06)
        first = lax.axis_index(("y", "z", "c")) * own
        own_weights = lax.dynamic_slice_in_dim(weights, first, own, 0)
        return own_weights - 0.5 * ratio[None, :, None] * own_grads

    return body


def solution(mesh):
    nx, ny, nz, nc = mesh.shape["dp"], 4, 16, 2
    grid = Mesh(mesh.devices.reshape(nx, ny, nz, nc), ("x", "y", "z", "c"))
    tokens = P("x", ("y", "z", "c"), None)
    return jax.shard_map(
        make_body(nx, ny, nz, nc),
        mesh=grid,
        in_specs=(tokens, tokens, tokens, tokens, P()),
        out_specs=P(("y", "z", "c"), None, None),
        check_vma=False,
    )
```

time: 518 us -> 109 us (0.21)
  waiting for transfers between devices: 471 us -> 7.75 us
  blocking collectives: 0 us -> 51.6 us
  starting transfers between devices: 0.01 us -> 16.9 us
  between operations: 13.6 us -> 0.23 us
    psum x1 -> x0, waiting for transfers between devices: 471 us -> none  [body(): lax.psum(jnp.stack([grad_k.reshape(rows_all, kv_count * HEAD), grad_v.res...]
    all_to_all x0 -> x3, blocking collectives: none -> 51.6 us  [the longest x1 25 us: body(): lax.all_to_all(plane.reshape(nz, 2 * own, part), 'z', 0, 0, tiled=True)]
    ppermute x0 -> x1, starting transfers between devices: none -> 8.78 us  [body(): half = mine + lax.ppermute(other, 'c', pairs)]
    all_to_all x0 -> x1, starting transfers between devices: none -> 8.08 us  [body(): lax.all_to_all(jnp.broadcast_to(packed[None], (count,) + packed.shape), (...]
    reshape x2 -> x1, local copies, waits for them, and re-layouts: 7.29 us -> 0.02 us  [body(): mean.reshape(nx, 2, own, part).transpose(2, 1, 0, 3).reshape(own, 2, width)]
    all_to_all x0 -> x1, waiting for transfers between devices: none -> 6.23 us  [body(): lax.all_to_all(jnp.broadcast_to(packed[None], (count,) + packed.shape), (...]
    unnamed x14 -> x17, local copies, waits for them, and re-layouts: 1.61 us -> 7.57 us
  transfers between devices with their start and end apart: 1 -> 2, of which waited for: 1 -> 2; matrix products, arithmetic and copies ran while one was open for 0% -> 1% of each run, Pallas kernels for 0% -> 0%
where the time goes in v1:
time: 109 us
  blocking collectives  51.6 us (47%)
  starting transfers between devices  16.9 us (16%)
  matrix products  15 us (14%)
  local copies, waits for them, and re-layouts  10.5 us (10%)
  waiting for transfers between devices  7.75 us (7%)
  other arithmetic  6.59 us (6%)
    all_to_all x1, blocking collectives, body(): lax.all_to_all(plane.reshape(nz, 2 * own, part), 'z', 0, 0, tiled=True)  25 us
    all_to_all x1, blocking collectives, body(): lax.all_to_all(jnp.broadcast_to(squares[None], (nz, 2, part)), 'z', 0, 0,...  13.8 us
    all_to_all x1, blocking collectives, body(): lax.all_to_all(half.reshape(nx * ny, rows, part), ('x', 'y'), 0, 0, tiled...  12.9 us
    dot_general x1, matrix products, local_grads(): jnp.einsum('rgjp,rgjd->pgd', dscores, q_local, preferred_element_type=jnp...  10.1 us
    ppermute x1, starting transfers between devices, body(): half = mine + lax.ppermute(other, 'c', pairs)  8.78 us
    all_to_all x1, starting transfers between devices, body(): lax.all_to_all(jnp.broadcast_to(packed[None], (count,) + packed.shape), (...  8.08 us
    unnamed x17, local copies, waits for them, and re-layouts  7.57 us
    all_to_all x1, waiting for transfers between devices, body(): lax.all_to_all(jnp.broadcast_to(packed[None], (count,) + packed.shape), (...  6.23 us
  transfers between devices with their start and end apart: 2, of which 2 were waited for; matrix products, arithmetic and copies ran while one was open for 1% of the time, Pallas kernels for 0%

profile of v1, /device:TPU:1, one launch (start us, length us, event | category | flops | bytes accessed | tf_op | source)
XLA Modules:
  0.0 108.5 jit_solution(14689436023268552981)
XLA Ops:
  0.0 2.2 %copy.111 = bf16[16,8,64,128]{3,2,1,0:T(8,128)(2,1)S(1)} copy(bf16[16,8,64,128]{3,1,2,0:T(8,128)(2,1)} %bitcast.91) | data formatting | bytes 4194304
  2.2 2.2 %fusion.39 = (bf16[256,1,512]{2,1,0:T(2,128)(2,1)S(1)}, bf16[256,1,512]{2,1,0:T(2,128)(2,1)S(1)}) fusion(bf16[256,2,512]{2,1,0:T(2,128)(2,1)} %param.9), kind=kLoop, calls=%fused_computation.42 | loop fusion | bytes 1048576 | tf_op jit(solution)/shard_map/slice | solution.py:20
  4.4 0.5 copy.107
  4.8 1.1 %copy.108 = bf16[256,1,512]{0,2,1:T(8,128)(2,1)} copy(bf16[256,1,512]{2,1,0:T(2,128)(2,1)S(1)} %get-tuple-element.7) | data formatting | bytes 524288
  6.0 3.6 %copy.112 = bf16[16,8,64,128]{3,2,1,0:T(8,128)(2,1)} copy(bf16[16,8,64,128]{3,1,2,0:T(8,128)(2,1)} %bitcast.92) | data formatting | bytes 4194304
  9.5 0.0 copy-start.4
  9.5 0.0 copy-start.2
  9.5 2.1 %bitcast_reduce_fusion = (f32[128,4,16]{0,2,1:T(8,128)S(1)}, f32[4,256,128,16]{2,1,3,0:T(8,128)S(1)}) fusion(bf16[256,4,128,1]{0,2,3,1:T(8,128)(2,1)S(1)} %bitcast.95, bf16[128,4,16,128]{3,2,1,0:T(8,128)(2,1)S(1)} %bitcast.88), kind=kOutput, calls=%fused_computation.5 | convolution fusion | flops 541057024 | bytes 10780672 | tf_op jit(solution)/shard_map/rgjd,pgd->rgjp/dot_general | solution.py:21
  11.7 0.0 copy-start
  11.7 0.0 copy-start.3
  11.7 0.0 copy-start.5
  11.7 2.0 %fusion.3 = f32[128,4,16]{0,2,1:T(8,128)S(1)} fusion(f32[4,256,128,16]{2,1,3,0:T(8,128)S(1)} %get-tuple-element.10, f32[128,4,16]{0,2,1:T(8,128)S(1)} %get-tuple-element.9), kind=kLoop, calls=%fused_computation.7 | loop fusion | flops 6283264 | bytes 8454144 | tf_op jit(solution)/shard_map/reduce_sum | solution.py:23
  13.7 0.0 copy-done.4
  13.8 0.0 copy-done.2
  13.8 2.7 %fusion.6 = f32[4,256,128,1]{2,1,3,0:T(8,128)S(1)} fusion(f32[4,256,128,16]{2,1,3,0:T(8,128)S(1)} %get-tuple-element.10, f32[128,4,16]{0,2,1:T(8,128)S(1)} %add_select_fusion, bf16[128,4,16,128]{3,2,1,0:T(8,128)(2,1)S(1)} %bitcast.94), kind=kOutput, calls=%fused_computation.10 | convolution fusion | flops 543162368 | bytes 11042816 | tf_op jit(solution)/shard_map/rgjp,rgjd->pgd/dot_general | solution.py:27
  16.5 0.0 copy-done
  16.5 0.0 copy-done.3
  16.5 0.0 copy-done.5
  16.5 0.0 copy-start.1
  16.5 10.1 %fusion.27 = f32[4,256,128]{2,1,0:T(8,128)} fusion(bf16[128,4,16,128]{3,2,1,0:T(8,128)(2,1)S(1)} %bitcast.89, f32[4,256,128,16]{2,1,3,0:T(8,128)} %copy-done, f32[128,4,16]{0,2,1:T(8,128)S(1)} %bitcast.106, f32[128,4,16]{0,2,1:T(8,128)S(1)} %add_select_fusion, bf16[256,4,128,1]{0,2,3,1:T(8,128)(2,1)S(1)} %bitcast.99, bf16[128,4,16,128]{3,2,1,0:T(8,128)(2,1)} %bitcast.93), kind=kOutput, calls=%fused_computation.21 | convolution fusion | flops 1084358656 | bytes 13434880 | tf_op jit(solution)/shard_map/rgjp,rgjd->pgd/dot_general | solution.py:30
  26.7 1.7 %fusion.35 = (f32[2,4,16,1,2,4,128]{6,4,3,2,1,5,0:T(2,128)S(1)}, f32[2,4,16,1,2,4,128]{6,4,3,2,1,5,0:T(2,128)S(1)}) fusion(s32[]{:T(128)S(6)} %select_n.23, f32[1,4,16,2,2,4,128]{6,4,3,2,1,5,0:T(2,128)} %bitcast.98, f32[1,4,16,2,2,4,128]{6,4,3,2,1,5,0:T(2,128)S(1)} %bitcast.97, s32[]{:T(128)S(6)} %select_n.24), kind=kLoop, calls=%fused_computation.28 | loop fusion | flops 262144 | bytes 2097160 | tf_op jit(solution)/shard_map/stack | solution.py:42
  28.4 0.2 copy.137
  28.6 8.8 %collective-permute-start = (f32[4,4,16,2,2,128]{5,4,3,2,1,0:T(2,128)S(1)}, f32[4,4,16,2,2,128]{5,4,3,2,1,0:T(2,128)S(1)}, u32[]{:S(2)}, u32[]{:S(2)}) collective-permute-start(f32[4,4,16,2,2,128]{5,4,3,2,1,0:T(2,128)S(1)} %bitcast.96), channel_id=1, source_target_pairs={{0,1},{1,0},{2,3},{3,2},{4,5},{5,4},{6,7},{7,6},{8,9},{9,8},{10,11... | collective-permute-start | bytes 1572872 | tf_op jit(solution)/shard_map/ppermute | solution.py:48
  37.4 1.5 %collective-permute-done = f32[4,4,16,2,2,128]{5,4,3,2,1,0:T(2,128)S(1)} collective-permute-done((f32[4,4,16,2,2,128]{5,4,3,2,1,0:T(2,128)S(1)}, f32[4,4,16,2,2,128]{5,4,3,2,1,0:T(2,128)S(1)}, u32[]{:S(2)}, u32[]{:S(2)}) %collective-permute-start) | collective-permute-done | bytes 524320 | tf_op jit(solution)/shard_map/ppermute | solution.py:48
  38.9 0.3 fusion.36
  39.2 12.9 %all_to_all.20 = f32[16,64,128]{2,1,0:T(8,128)S(1)} all-to-all(f32[16,64,128]{2,1,0:T(8,128)S(1)} %bitcast.90), channel_id=1, replica_groups=mesh['x'=4,'y'=4,'z'=16,'c'=2] {'x','y'}, dimensions={0} | all-to-all | bytes 1048576 | tf_op jit(solution)/shard_map/all_to_all | solution.py:50
  52.1 25.0 %all_to_all.21 = f32[16,4,128]{2,1,0:T(4,128)S(1)} all-to-all(f32[16,4,128]{2,1,0:T(4,128)S(1)} %bitcast.100), channel_id=1, replica_groups=mesh['x'=4,'y'=4,'z'=16,'c'=2] {'z'}, dimensions={0} | all-to-all | bytes 65536 | tf_op jit(solution)/shard_map/all_to_all | solution.py:53
  77.2 13.8 %all_to_all.22 = f32[16,2,128]{2,1,0:T(2,128)S(1)} all-to-all(f32[16,2,128]{2,1,0:T(2,128)S(1)} %broadcast_in_dim.4), channel_id=1, replica_groups=mesh['x'=4,'y'=4,'z'=16,'c'=2] {'z'}, dimensions={0} | all-to-all | bytes 32768 | tf_op jit(solution)/shard_map/all_to_all | solution.py:57
  91.0 0.6 broadcast_in_dim.5
  91.7 8.1 %all-to-all-start.3 = ((f32[32,6,128]{2,1,0:T(8,128)}), f32[32,6,128]{2,1,0:T(8,128)S(1)}, u32[]{:S(2)}, u32[]{:S(2)}) async-start(f32[32,6,128]{2,1,0:T(8,128)} %broadcast_in_dim.5), calls=%async_computation.3 | async-start | bytes 262144 | tf_op jit(solution)/shard_map/all_to_all | solution.py:62
  99.7 0.0 copy-done.1
  99.8 1.2 %multiply_reduce_fusion = f32[2]{0:T(128)S(1)} fusion(bf16[256,2,512]{2,1,0:T(2,128)(2,1)S(1)} %copy-done.1), kind=kLoop, calls=%fused_computation.26 | loop fusion | flops 786430 | bytes 524296 | tf_op jit(solution)/shard_map/reduce_sum | solution.py:72
  101.0 0.4 convert_element_type.9
  101.3 6.2 %all-to-all-done.3 = f32[32,6,128]{2,1,0:T(8,128)S(1)} async-done(((f32[32,6,128]{2,1,0:T(8,128)}), f32[32,6,128]{2,1,0:T(8,128)S(1)}, u32[]{:S(2)}, u32[]{:S(2)}) %all-to-all-start.3) | async-done | bytes 98336 | tf_op jit(solution)/shard_map/all_to_all | solution.py:62
  107.7 0.1 slice_reduce_fusion
  107.8 0.7 multiply_subtract_fusion
  (15 shorter events, 0.3 us)
Async XLA Ops:
  9.5 4.2 %copy-start.4 = (f32[1,128,64]{1,2,0:T(8,128)S(1)}, f32[1,128,64]{1,2,0:T(8,128)}, u32[]{:S(2)}) copy-start(f32[1,128,64]{1,2,0:T(8,128)} %param.7) | copy-start | bytes 98308
  9.5 4.2 %copy-start.2 = (bf16[16,8,64,128]{3,2,1,0:T(8,128)(2,1)S(1)}, bf16[16,8,64,128]{3,2,1,0:T(8,128)(2,1)}, u32[]{:S(2)}) copy-start(bf16[16,8,64,128]{3,2,1,0:T(8,128)(2,1)} %copy.112) | copy-start | bytes 6291460
  11.7 4.8 %copy-start = (f32[4,256,128,16]{2,1,3,0:T(8,128)}, f32[4,256,128,16]{2,1,3,0:T(8,128)S(1)}, u32[]{:S(2)}) copy-start(f32[4,256,128,16]{2,1,3,0:T(8,128)S(1)} %get-tuple-element.10) | copy-start | bytes 25165828
  11.7 4.8 %copy-start.3 = (bf16[256,1,512]{0,2,1:T(8,128)(2,1)S(1)}, bf16[256,1,512]{0,2,1:T(8,128)(2,1)}, u32[]{:S(2)}) copy-start(bf16[256,1,512]{0,2,1:T(8,128)(2,1)} %copy.108) | copy-start | bytes 786436
  11.7 4.8 %copy-start.5 = (f32[1,128,64]{1,2,0:T(8,128)S(1)}, f32[1,128,64]{1,2,0:T(8,128)}, u32[]{:S(2)}) copy-start(f32[1,128,64]{1,2,0:T(8,128)} %param.8) | copy-start | bytes 98308
  16.5 83.2 %copy-start.1 = (bf16[256,2,512]{2,1,0:T(2,128)(2,1)S(1)}, bf16[256,2,512]{2,1,0:T(2,128)(2,1)}, u32[]{:S(2)}) copy-start(bf16[256,2,512]{2,1,0:T(2,128)(2,1)} %param.9) | copy-start | bytes 1572868
  28.6 10.3 %collective-permute-start = (f32[4,4,16,2,2,128]{5,4,3,2,1,0:T(2,128)S(1)}, f32[4,4,16,2,2,128]{5,4,3,2,1,0:T(2,128)S(1)}, u32[]{:S(2)}, u32[]{:S(2)}) collective-permute-start(f32[4,4,16,2,2,128]{5,4,3,2,1,0:T(2,128)S(1)} %bitcast.96), channel_id=1, source_target_pairs={{0,1},{1,0},{2,3},{3,2},{4,5},{5,4},{6,7},{7,6},{8,9},{9,8},{10,11... | collective-permute-start | bytes 1572872 | tf_op jit(solution)/shard_map/ppermute | solution.py:48
  91.7 15.9 %all-to-all-start.3 = ((f32[32,6,128]{2,1,0:T(8,128)}), f32[32,6,128]{2,1,0:T(8,128)S(1)}, u32[]{:S(2)}, u32[]{:S(2)}) async-start(f32[32,6,128]{2,1,0:T(8,128)} %broadcast_in_dim.5), calls=%async_computation.3 | async-start | bytes 262144 | tf_op jit(solution)/shard_map/all_to_all | solution.py:62

commit v2 on v1

v2 whole, which is shorter than its diff:
```python
import functools

import jax
import jax.numpy as jnp
from jax import lax
from jax.experimental import pallas as pl
from jax.experimental.pallas import tpu as pltpu
from jax.sharding import Mesh, PartitionSpec as P

HEAD = 128
SCALE = HEAD ** (-0.5)
LOG2E = 1.4426950408889634
NT = (((1,), (1,)), ((), ()))
NN = (((1,), (0,)), ((), ()))
F32 = jnp.float32


def grads_kernel(
    ny, nz, core_ref, low_ref, q_ref, d_ref, lse_ref, dot_ref, send_ref, own_ref, sq_ref, w_ref
):
    group = pl.program_id(0)
    core = core_ref[0]
    heads = lse_ref.shape[0]

    @pl.when(group == 0)
    def _():
        w_ref[...] = low_ref[...].astype(F32)
        sq_ref[...] = jnp.zeros_like(sq_ref)

    sides = []
    for kv in range(2):
        rows = []
        total = jnp.zeros((8, HEAD), F32)
        for half in (1 - core, core):
            for y in range(ny):
                for r in range(2):
                    first = y * nz * 32 + half * 16 + r * 8 + group * 2 + kv
                    block = w_ref[pl.ds(first, nz, stride=32), :]
                    total += (block * block).reshape(nz // 8, 8, HEAD).sum(0)
                    rows.append(block)
        sides.append(jnp.concatenate(rows, 0).astype(jnp.bfloat16))
        sq_ref[kv] += total
    keys, values = sides

    q = jnp.concatenate([q_ref[:, h * HEAD : (h + 1) * HEAD] for h in range(heads)], 0)
    d = jnp.concatenate([d_ref[:, h * HEAD : (h + 1) * HEAD] for h in range(heads)], 0)
    lse = jnp.concatenate([lse_ref[h : h + 1, :] for h in range(heads)], 1) * LOG2E
    dot = jnp.concatenate([dot_ref[h : h + 1, :] for h in range(heads)], 1)
    scores = lax.dot_general(keys, q, NT, preferred_element_type=F32)
    top = jnp.maximum(jnp.max(scores, axis=0, keepdims=True) * (SCALE * LOG2E), lse)
    probs = jnp.exp2(scores * (SCALE * LOG2E) - top)
    probs = probs * (1.0 / (jnp.sum(probs, axis=0, keepdims=True) + jnp.exp2(lse - top)))
    dprobs = lax.dot_general(values, d, NT, preferred_element_type=F32)
    dscores = (probs * (dprobs - dot)).astype(jnp.bfloat16)
    grad_v = lax.dot_general(probs.astype(jnp.bfloat16), d, NN, preferred_element_type=F32)
    grad_k = lax.dot_general(dscores, q, NN, preferred_element_type=F32) * SCALE
    at = 0
    for ref in (send_ref, own_ref):
        for y in range(ny):
            for r in range(2):
                ref[0, y, pl.ds(r, nz, stride=4), :] = grad_k[at : at + nz]
                ref[0, y, pl.ds(2 + r, nz, stride=4), :] = grad_v[at : at + nz]
                at += nz


def local_grads(nx, ny, nz, core, weights, queries, grad_out, seq_lse, out_dot):
    tok, cols = queries.shape
    heads = seq_lse.shape[0] // nx
    half = jax.ShapeDtypeStruct((nx, ny, nz * 4, HEAD), F32)
    spec = pl.BlockSpec((1, ny, nz * 4, HEAD), lambda g: (g, 0, 0, 0))
    return pl.pallas_call(
        functools.partial(grads_kernel, ny, nz),
        grid=(nx,),
        in_specs=[
            pl.BlockSpec(memory_space=pltpu.SMEM),
            pl.BlockSpec(weights.shape, lambda g: (0, 0)),
            pl.BlockSpec((tok, cols // nx), lambda g: (0, g)),
            pl.BlockSpec((tok, cols // nx), lambda g: (0, g)),
            pl.BlockSpec((heads, tok), lambda g: (g, 0)),
            pl.BlockSpec((heads, tok), lambda g: (g, 0)),
        ],
        out_specs=[spec, spec, pl.BlockSpec((2, 8, HEAD), lambda g: (0, 0, 0))],
        out_shape=[half, half, jax.ShapeDtypeStruct((2, 8, HEAD), F32)],
        scratch_shapes=[pltpu.VMEM(weights.shape, F32)],
        compiler_params=pltpu.CompilerParams(vmem_limit_bytes=60 * 2**20),
        name="prefix_grads",
    )(core, weights, queries, grad_out, seq_lse, out_dot)


def make_body(nx, ny, nz, nc):
    def body(queries, grad_out, seq_lse, out_dot, prefix):
        rows_all, width = prefix.shape[0], prefix.shape[2]
        own = rows_all // (ny * nz * nc)
        part = width // nx
        core = lax.axis_index("c")
        weights = prefix.reshape(rows_all, 2, nx, part).transpose(0, 2, 1, 3).reshape(-1, part)
        send, mine, w_squares = local_grads(
            nx, ny, nz, core.reshape(1), weights, queries[0], grad_out[0], seq_lse[0].T, out_dot[0].T
        )
        half = mine + lax.ppermute(send, "c", [(i, (i + 1) % nc) for i in range(nc)])
        rows = nz * 2 * own
        plane = lax.all_to_all(
            half.reshape(nx * ny, rows, part), ("x", "y"), 0, 0, tiled=True
        ).sum(0)
        piece = lax.all_to_all(
            plane.reshape(nz, 2 * own, part), "z", 0, 0, tiled=True
        ).sum(0)
        squares = (piece * piece).reshape(2, own, part).sum(1)
        squares = lax.all_to_all(
            jnp.broadcast_to(squares[None], (nz, 2, part)), "z", 0, 0, tiled=True
        ).sum(0)
        packed = jnp.concatenate([piece, squares], 0)
        count = nx * ny * nc
        packed = lax.all_to_all(
            jnp.broadcast_to(packed[None], (count,) + packed.shape),
            ("x", "y", "c"), 0, 0, tiled=True,
        )
        grad_ms = packed[:, 2 * own :].sum((0, 2)) / (rows_all * width)
        packed = packed.reshape(nx, ny * nc, 2 * own + 2, part)
        place = lax.axis_index("y") * nc + core
        mean = lax.dynamic_index_in_dim(packed, place, 1, keepdims=False)[:, : 2 * own]
        own_grads = mean.reshape(nx, 2, own, part).transpose(2, 1, 0, 3).reshape(own, 2, width)
        weight_ms = w_squares.sum((1, 2)) / (rows_all * width)
        ratio = jnp.sqrt(weight_ms) / jnp.sqrt(grad_ms + 1e-06)
        first = lax.axis_index(("y", "z", "c")) * own
        own_weights = lax.dynamic_slice_in_dim(prefix, first, own, 0).astype(F32)
        return own_weights - 0.5 * ratio[None, :, None] * own_grads

    return body


def solution(mesh):
    nx, ny, nz, nc = mesh.shape["dp"], 4, 16, 2
    grid = Mesh(mesh.devices.reshape(nx, ny, nz, nc), ("x", "y", "z", "c"))
    tokens = P("x", ("y", "z", "c"), None)
    return jax.shard_map(
        make_body(nx, ny, nz, nc),
        mesh=grid,
        in_specs=(tokens, tokens, tokens, tokens, P()),
        out_specs=P(("y", "z", "c"), None, None),
        check_vma=False,
    )
```

time: 109 us -> 91.7 us (0.84)
  matrix products: 15 us -> 0 us
  local copies, waits for them, and re-layouts: 10.5 us -> 0.73 us
  Pallas kernels: 0 us -> 9.61 us
  other arithmetic: 6.59 us -> 2.87 us
  waiting for transfers between devices: 7.75 us -> 9.42 us
    dot_general x3 -> x0, matrix products: 15 us -> none  [the longest x1 10.1 us: local_grads(): jnp.einsum('rgjp,rgjd->pgd', dscores, q_local, preferred_element_type=jnp...]
    pallas_call x0 -> x1, Pallas kernels: none -> 9.61 us  [local_grads(): pl.pallas_call(functools.partial(grads_kernel, ny, nz), grid=(nx,), in_sp...]
    unnamed x17 -> x2, local copies, waits for them, and re-layouts: 7.57 us -> 0.01 us
    reduce_sum x2 -> x1, other arithmetic: 3.19 us -> 0.1 us  [body(): weight_ms = w_squares.sum((1, 2)) / (rows_all * width)]
    slice x1 -> x0, local copies, waits for them, and re-layouts: 2.16 us -> none  [local_grads(): values = prefix[:, 1, :].reshape(rows_all, kv_count, HEAD)]
    another operation x1 -> x0, other arithmetic: 1.72 us -> none  [body(): grads = jnp.stack([grad_k, grad_v], 0).reshape(2, ny, nz, nc, own, nx, part)]
    all_to_all x1, waiting for transfers between devices: 6.23 us -> 7.69 us  [body(): lax.all_to_all(jnp.broadcast_to(packed[None], (count,) + packed.shape), (...]
  transfers between devices with their start and end apart: 2 -> 2, of which waited for: 2 -> 2; matrix products, arithmetic and copies ran while one was open for 1% -> 0% of each run, Pallas kernels for 0% -> 0%
where the time goes in v2:
time: 91.7 us; the launch traced here: 91.3 us
  blocking collectives  51.6 us (56%)
  starting transfers between devices  17 us (19%)
  Pallas kernels  9.61 us (10%)
  waiting for transfers between devices  9.42 us (10%)
  other arithmetic  2.87 us (3%)
    all_to_all x1, blocking collectives, body(): lax.all_to_all(plane.reshape(nz, 2 * own, part), 'z', 0, 0, tiled=True)  25 us
    all_to_all x1, blocking collectives, body(): lax.all_to_all(jnp.broadcast_to(squares[None], (nz, 2, part)), 'z', 0, 0,...  13.8 us
    all_to_all x1, blocking collectives, body(): lax.all_to_all(half.reshape(nx * ny, rows, part), ('x', 'y'), 0, 0, tiled...  12.9 us
    pallas_call x1, Pallas kernels, local_grads(): pl.pallas_call(functools.partial(grads_kernel, ny, nz), grid=(nx,), in_sp...  9.61 us
    ppermute x1, starting transfers between devices, body(): lax.ppermute(send, 'c', [(i, (i + 1) % nc) for i in range(nc)])  8.89 us
    all_to_all x1, starting transfers between devices, body(): lax.all_to_all(jnp.broadcast_to(packed[None], (count,) + packed.shape), (...  8.07 us
    all_to_all x1, waiting for transfers between devices, body(): lax.all_to_all(jnp.broadcast_to(packed[None], (count,) + packed.shape), (...  7.69 us
  transfers between devices with their start and end apart: 2, of which 2 were waited for; matrix products, arithmetic and copies ran while one was open for 0% of the time, Pallas kernels for 0%

profile of v2, /device:TPU:1, one launch (start us, length us, event | category | flops | bytes accessed | tf_op | source)
XLA Modules:
  0.0 91.3 jit_solution(17731460286396652754)
XLA Ops:
  0.0 9.6 %prefix_grads.1 = (f32[4,4,64,128]{3,2,1,0:T(8,128)}, f32[4,4,64,128]{3,2,1,0:T(8,128)}, f32[2,8,128]{2,1,0:T(8,128)}) custom-call(s32[1]{0:T(128)} %bitcast.core_ref, bf16[2048,128]{1,0:T(8,128)(2,1)} %bitcast.27, bf16[128,8192]{1,0:T(8,128)(2,1)} %bitcast.24, bf16[128,8192]{1,0:T(8,128)(2,1)} %bitcast.25, f32[64,128]{1,0:T(8,128)} %bitcast.31, ...), custom_call_target="tpu_custom_call" | custom-call | tf_op jit(solution)/shard_map/prefix_grads/pallas_call | solution.py:71
  9.6 0.0 copy-start
  9.6 8.9 %collective-permute-start = (f32[4,4,64,128]{3,2,1,0:T(8,128)}, f32[4,4,64,128]{3,2,1,0:T(8,128)S(1)}, u32[]{:S(2)}, u32[]{:S(2)}) collective-permute-start(f32[4,4,64,128]{3,2,1,0:T(8,128)} %get-tuple-element.10), channel_id=1, source_target_pairs={{0,1},{1,0},{2,3},{3,2},{4,5},{5,4},{6,7},{7,6},{8,9},{9,8},{10,11... | collective-permute-start | bytes 1572872 | tf_op jit(solution)/shard_map/ppermute | solution.py:100
  18.5 1.7 %collective-permute-done = f32[4,4,64,128]{3,2,1,0:T(8,128)S(1)} collective-permute-done((f32[4,4,64,128]{3,2,1,0:T(8,128)}, f32[4,4,64,128]{3,2,1,0:T(8,128)S(1)}, u32[]{:S(2)}, u32[]{:S(2)}) %collective-permute-start) | collective-permute-done | bytes 524320 | tf_op jit(solution)/shard_map/ppermute | solution.py:100
  20.2 1.1 %add.29 = f32[4,4,64,128]{3,2,1,0:T(8,128)S(1)} add(f32[4,4,64,128]{3,2,1,0:T(8,128)} %get-tuple-element.9, f32[4,4,64,128]{3,2,1,0:T(8,128)S(1)} %collective-permute-done) | non-fusion elementwise | flops 131072 | bytes 1572864 | tf_op jit(solution)/shard_map/add | solution.py:100
  21.4 12.9 %all_to_all.20 = f32[16,64,128]{2,1,0:T(8,128)S(1)} all-to-all(f32[16,64,128]{2,1,0:T(8,128)S(1)} %bitcast.26), channel_id=1, replica_groups=mesh['x'=4,'y'=4,'z'=16,'c'=2] {'x','y'}, dimensions={0} | all-to-all | bytes 1048576 | tf_op jit(solution)/shard_map/all_to_all | solution.py:102
  34.3 25.0 %all_to_all.21 = f32[16,4,128]{2,1,0:T(4,128)S(1)} all-to-all(f32[16,4,128]{2,1,0:T(4,128)S(1)} %bitcast.28), channel_id=1, replica_groups=mesh['x'=4,'y'=4,'z'=16,'c'=2] {'z'}, dimensions={0} | all-to-all | bytes 65536 | tf_op jit(solution)/shard_map/all_to_all | solution.py:105
  59.3 13.8 %all_to_all.22 = f32[16,2,128]{2,1,0:T(2,128)S(1)} all-to-all(f32[16,2,128]{2,1,0:T(2,128)S(1)} %broadcast_in_dim.4), channel_id=1, replica_groups=mesh['x'=4,'y'=4,'z'=16,'c'=2] {'z'}, dimensions={0} | all-to-all | bytes 32768 | tf_op jit(solution)/shard_map/all_to_all | solution.py:109
  73.1 0.6 broadcast_in_dim.5
  73.8 8.1 %all-to-all-start.3 = ((f32[32,6,128]{2,1,0:T(8,128)}), f32[32,6,128]{2,1,0:T(8,128)S(1)}, u32[]{:S(2)}, u32[]{:S(2)}) async-start(f32[32,6,128]{2,1,0:T(8,128)} %broadcast_in_dim.5), calls=%async_computation.3 | async-start | bytes 262144 | tf_op jit(solution)/shard_map/all_to_all | solution.py:114
  81.9 0.0 copy-done
  81.9 0.1 reduce_sum.54
  82.0 7.7 %all-to-all-done.3 = f32[32,6,128]{2,1,0:T(8,128)S(1)} async-done(((f32[32,6,128]{2,1,0:T(8,128)}), f32[32,6,128]{2,1,0:T(8,128)S(1)}, u32[]{:S(2)}, u32[]{:S(2)}) %all-to-all-start.3) | async-done | bytes 98336 | tf_op jit(solution)/shard_map/all_to_all | solution.py:114
  89.8 0.1 slice_reduce_fusion
  89.9 1.4 %multiply_subtract_fusion = f32[2,2,512]{2,1,0:T(2,128)} fusion(f32[2,2,512]{2,1,0:T(2,128)S(1)} %reshape.48, f32[2]{0:T(128)S(1)} %multiply_multiply_fusion, bf16[256,2,512]{2,1,0:T(2,128)(2,1)} %param.9, s32[]{:T(128)S(6)} %select_n.7), kind=kLoop, calls=%fused_computation.2 | loop fusion | flops 6144 | bytes 20492 | tf_op jit(solution)/shard_map/sub | solution.py:127
  (14 shorter events, 0.2 us)
Async XLA Ops:
  9.6 72.3 %copy-start = (f32[2,8,128]{2,1,0:T(8,128)S(1)}, f32[2,8,128]{2,1,0:T(8,128)}, u32[]{:S(2)}) copy-start(f32[2,8,128]{2,1,0:T(8,128)} %get-tuple-element.8) | copy-start | bytes 24580
  9.6 10.6 %collective-permute-start = (f32[4,4,64,128]{3,2,1,0:T(8,128)}, f32[4,4,64,128]{3,2,1,0:T(8,128)S(1)}, u32[]{:S(2)}, u32[]{:S(2)}) collective-permute-start(f32[4,4,64,128]{3,2,1,0:T(8,128)} %get-tuple-element.10), channel_id=1, source_target_pairs={{0,1},{1,0},{2,3},{3,2},{4,5},{5,4},{6,7},{7,6},{8,9},{9,8},{10,11... | collective-permute-start | bytes 1572872 | tf_op jit(solution)/shard_map/ppermute | solution.py:100
  73.8 15.9 %all-to-all-start.3 = ((f32[32,6,128]{2,1,0:T(8,128)}), f32[32,6,128]{2,1,0:T(8,128)S(1)}, u32[]{:S(2)}, u32[]{:S(2)}) async-start(f32[32,6,128]{2,1,0:T(8,128)} %broadcast_in_dim.5), calls=%async_computation.3 | async-start | bytes 262144 | tf_op jit(solution)/shard_map/all_to_all | solution.py:114

commit v3 on v2

--- a/solution.py
+++ b/solution.py
@@ -16,16 +16,19 @@
 
 
 def grads_kernel(
-    ny, nz, core_ref, low_ref, q_ref, d_ref, lse_ref, dot_ref, send_ref, own_ref, sq_ref, w_ref
+    ny, nz, at_ref, low_ref, q_ref, d_ref, lse_ref, dot_ref,
+    send_ref, own_ref, sq_ref, own_w_ref, w_ref,
 ):
     group = pl.program_id(0)
-    core = core_ref[0]
+    core = at_ref[0]
     heads = lse_ref.shape[0]
 
     @pl.when(group == 0)
     def _():
         w_ref[...] = low_ref[...].astype(F32)
         sq_ref[...] = jnp.zeros_like(sq_ref)
+        start = pl.multiple_of(at_ref[1] * 8, 8)
+        own_w_ref[...] = w_ref[pl.ds(start, own_w_ref.shape[0]), :]
 
     sides = []
     for kv in range(2):
@@ -63,7 +66,7 @@
                 at += nz
 
 
-def local_grads(nx, ny, nz, core, weights, queries, grad_out, seq_lse, out_dot):
+def local_grads(nx, ny, nz, own, place, weights, queries, grad_out, seq_lse, out_dot):
     tok, cols = queries.shape
     heads = seq_lse.shape[0] // nx
     half = jax.ShapeDtypeStruct((nx, ny, nz * 4, HEAD), F32)
@@ -79,64 +82,77 @@
             pl.BlockSpec((heads, tok), lambda g: (g, 0)),
             pl.BlockSpec((heads, tok), lambda g: (g, 0)),
         ],
-        out_specs=[spec, spec, pl.BlockSpec((2, 8, HEAD), lambda g: (0, 0, 0))],
-        out_shape=[half, half, jax.ShapeDtypeStruct((2, 8, HEAD), F32)],
+        out_specs=[
+            spec,
+            spec,
+            pl.BlockSpec((2, 8, HEAD), lambda g: (0, 0, 0)),
+            pl.BlockSpec((own * 8, HEAD), lambda g: (0, 0)),
+        ],
+        out_shape=[
+            half,
+            half,
+            jax.ShapeDtypeStruct((2, 8, HEAD), F32),
+            jax.ShapeDtypeStruct((own * 8, HEAD), F32),
+        ],
         scratch_shapes=[pltpu.VMEM(weights.shape, F32)],
         compiler_params=pltpu.CompilerParams(vmem_limit_bytes=60 * 2**20),
         name="prefix_grads",
-    )(core, weights, queries, grad_out, seq_lse, out_dot)
+    )(place, weights, queries, grad_out, seq_lse, out_dot)
 
 
-def make_body(nx, ny, nz, nc):
+def make_body(nx, ny, nh, nl, nc):
+    nz = nh * nl
+
+    def exchange(block, axes):
+        return lax.all_to_all(block, axes, 0, 0, tiled=True)
+
+    def to_all(block, axes, count):
+        return exchange(jnp.broadcast_to(block[None], (count,) + block.shape), axes)
+
     def body(queries, grad_out, seq_lse, out_dot, prefix):
         rows_all, width = prefix.shape[0], prefix.shape[2]
         own = rows_all // (ny * nz * nc)
         part = width // nx
         core = lax.axis_index("c")
+        first = lax.axis_index(("y", "h", "l", "c")) * own
         weights = prefix.reshape(rows_all, 2, nx, part).transpose(0, 2, 1, 3).reshape(-1, part)
-        send, mine, w_squares = local_grads(
-            nx, ny, nz, core.reshape(1), weights, queries[0], grad_out[0], seq_lse[0].T, out_dot[0].T
+        send, mine, w_squares, own_weights = local_grads(
+            nx, ny, nz, own, jnp.stack([core, first]), weights,
+            queries[0], grad_out[0], seq_lse[0].T, out_dot[0].T,
         )
         half = mine + lax.ppermute(send, "c", [(i, (i + 1) % nc) for i in range(nc)])
-        rows = nz * 2 * own
-        plane = lax.all_to_all(
-            half.reshape(nx * ny, rows, part), ("x", "y"), 0, 0, tiled=True
-        ).sum(0)
-        piece = lax.all_to_all(
-            plane.reshape(nz, 2 * own, part), "z", 0, 0, tiled=True
-        ).sum(0)
-        squares = (piece * piece).reshape(2, own, part).sum(1)
-        squares = lax.all_to_all(
-            jnp.broadcast_to(squares[None], (nz, 2, part)), "z", 0, 0, tiled=True
-        ).sum(0)
-        packed = jnp.concatenate([piece, squares], 0)
-        count = nx * ny * nc
-        packed = lax.all_to_all(
-            jnp.broadcast_to(packed[None], (count,) + packed.shape),
-            ("x", "y", "c"), 0, 0, tiled=True,
+        rows = 2 * own
+        plane = exchange(half.reshape(nx * ny, nz * rows, part), ("x", "y")).sum(0)
+        plane = plane.reshape(nh, nl, rows, part).transpose(1, 0, 2, 3)
+        plane = jnp.broadcast_to(plane[None], (nh,) + plane.shape).reshape(nz, nh * rows, part)
+        piece = exchange(plane, ("h", "l")).sum(0).reshape(nh, 2, own, part)
+        squares = (piece * piece).sum((0, 2))
+        piece = lax.dynamic_index_in_dim(piece, lax.axis_index("h"), 0, keepdims=False)
+        packed = jnp.concatenate(
+            [piece.reshape(rows, part), squares, jnp.zeros((8 - rows - 2, part), F32)], 0
         )
-        grad_ms = packed[:, 2 * own :].sum((0, 2)) / (rows_all * width)
-        packed = packed.reshape(nx, ny * nc, 2 * own + 2, part)
-        place = lax.axis_index("y") * nc + core
-        mean = lax.dynamic_index_in_dim(packed, place, 1, keepdims=False)[:, : 2 * own]
-        own_grads = mean.reshape(nx, 2, own, part).transpose(2, 1, 0, 3).reshape(own, 2, width)
+        packed = to_all(packed, ("x", "c"), nx * nc)
+        squares = packed[:, rows : rows + 2].sum(0)
+        packed = packed[:, :rows].reshape(nx, nc, 2, own, part)
+        own_grads = lax.dynamic_index_in_dim(packed, core, 1, keepdims=False)
+        grad_ms = to_all(squares, ("y", "l"), ny * nl).sum((0, 2)) / (rows_all * width)
         weight_ms = w_squares.sum((1, 2)) / (rows_all * width)
         ratio = jnp.sqrt(weight_ms) / jnp.sqrt(grad_ms + 1e-06)
-        first = lax.axis_index(("y", "z", "c")) * own
-        own_weights = lax.dynamic_slice_in_dim(prefix, first, own, 0).astype(F32)
+        own_grads = own_grads.transpose(2, 1, 0, 3).reshape(own, 2, width)
+        own_weights = own_weights.reshape(own, nx, 2, part).transpose(0, 2, 1, 3).reshape(own, 2, width)
         return own_weights - 0.5 * ratio[None, :, None] * own_grads
 
     return body
 
 
 def solution(mesh):
-    nx, ny, nz, nc = mesh.shape["dp"], 4, 16, 2
-    grid = Mesh(mesh.devices.reshape(nx, ny, nz, nc), ("x", "y", "z", "c"))
-    tokens = P("x", ("y", "z", "c"), None)
+    nx, ny, nh, nl, nc = mesh.shape["dp"], 4, 4, 4, 2
+    grid = Mesh(mesh.devices.reshape(nx, ny, nh, nl, nc), ("x", "y", "h", "l", "c"))
+    tokens = P("x", ("y", "h", "l", "c"), None)
     return jax.shard_map(
-        make_body(nx, ny, nz, nc),
+        make_body(nx, ny, nh, nl, nc),
         mesh=grid,
         in_specs=(tokens, tokens, tokens, tokens, P()),
-        out_specs=P(("y", "z", "c"), None, None),
+        out_specs=P(("y", "h", "l", "c"), None, None),
         check_vma=False,
     )

time: 91.7 us -> 86.2 us (0.940)
  blocking collectives: 51.6 us -> 12.9 us
  starting transfers between devices: 17 us -> 33.3 us
  waiting for transfers between devices: 9.42 us -> 25 us
  local copies, waits for them, and re-layouts: 0.73 us -> 2.02 us
    all_to_all x3 -> x1, blocking collectives: 51.6 us -> 12.9 us  [exchange(): return lax.all_to_all(block, axes, 0, 0, tiled=True)]
    all_to_all x1 -> x3, starting transfers between devices: 8.07 us -> 24.4 us  [exchange(): return lax.all_to_all(block, axes, 0, 0, tiled=True)]
    all_to_all x1 -> x3, waiting for transfers between devices: 7.69 us -> 23.3 us  [exchange(): return lax.all_to_all(block, axes, 0, 0, tiled=True)]
    broadcast_in_dim x2 -> x4, local copies, waits for them, and re-layouts: 0.66 us -> 1.87 us  [the longest x2 1.21 us: to_all(): return exchange(jnp.broadcast_to(block[None], (count,) + block.shape), axes)]
  transfers between devices with their start and end apart: 2 -> 4, of which waited for: 2 -> 4; matrix products, arithmetic and copies ran while one was open for 0% -> 0% of each run, Pallas kernels for 0% -> 0%
where the time goes in v3:
time: 86.2 us; the launch traced here: 85.8 us
  starting transfers between devices  33.3 us (39%)
  waiting for transfers between devices  25 us (29%)
  blocking collectives  12.9 us (15%)
  Pallas kernels  9.65 us (11%)
  other arithmetic  2.81 us (3%)
  local copies, waits for them, and re-layouts  2.02 us (2%)
    all_to_all x3, starting transfers between devices, exchange(): return lax.all_to_all(block, axes, 0, 0, tiled=True)  24.4 us
    all_to_all x3, waiting for transfers between devices, exchange(): return lax.all_to_all(block, axes, 0, 0, tiled=True)  23.3 us
    all_to_all x1, blocking collectives, exchange(): return lax.all_to_all(block, axes, 0, 0, tiled=True)  12.9 us
    pallas_call x1, Pallas kernels, local_grads(): pl.pallas_call(functools.partial(grads_kernel, ny, nz), grid=(nx,), in_sp...  9.65 us
    ppermute x1, starting transfers between devices, body(): lax.ppermute(send, 'c', [(i, (i + 1) % nc) for i in range(nc)])  8.9 us
    ppermute x1, waiting for transfers between devices, body(): lax.ppermute(send, 'c', [(i, (i + 1) % nc) for i in range(nc)])  1.73 us
  transfers between devices with their start and end apart: 4, of which 4 were waited for; matrix products, arithmetic and copies ran while one was open for 0% of the time, Pallas kernels for 0%

profile of v3, /device:TPU:1, one launch (start us, length us, event | category | flops | bytes accessed | tf_op | source)
XLA Modules:
  0.0 85.8 jit_solution(17534854103751599298)
XLA Ops:
  0.0 0.6 pad_add_fusion.at_ref
  0.6 9.6 %prefix_grads.1 = (f32[4,4,64,128]{3,2,1,0:T(8,128)}, f32[4,4,64,128]{3,2,1,0:T(8,128)}, f32[2,8,128]{2,1,0:T(8,128)}, f32[16,128]{1,0:T(8,128)}) custom-call(s32[2]{0:T(128)} %pad_add_fusion.at_ref, bf16[2048,128]{1,0:T(8,128)(2,1)} %bitcast.36, bf16[128,8192]{1,0:T(8,128)(2,1)} %bitcast.33, bf16[128,8192]{1,0:T(8,128)(2,1)} %bitcast.34, ...), custom_call_target="tpu_custom_call" | custom-call | tf_op jit(solution)/shard_map/prefix_grads/pallas_call | solution.py:74
  10.3 0.0 copy-start.1
  10.3 0.0 copy-start
  10.3 8.9 %collective-permute-start = (f32[4,4,64,128]{3,2,1,0:T(8,128)}, f32[4,4,64,128]{3,2,1,0:T(8,128)S(1)}, u32[]{:S(2)}, u32[]{:S(2)}) collective-permute-start(f32[4,4,64,128]{3,2,1,0:T(8,128)} %get-tuple-element.12), channel_id=1, source_target_pairs={{0,1},{1,0},{2,3},{3,2},{4,5},{5,4},{6,7},{7,6},{8,9},{9,8},{10,11... | collective-permute-start | bytes 1572872 | tf_op jit(solution)/shard_map/ppermute | solution.py:123
  19.2 1.7 %collective-permute-done = f32[4,4,64,128]{3,2,1,0:T(8,128)S(1)} collective-permute-done((f32[4,4,64,128]{3,2,1,0:T(8,128)}, f32[4,4,64,128]{3,2,1,0:T(8,128)S(1)}, u32[]{:S(2)}, u32[]{:S(2)}) %collective-permute-start) | collective-permute-done | bytes 524320 | tf_op jit(solution)/shard_map/ppermute | solution.py:123
  20.9 1.1 %add.30 = f32[4,4,64,128]{3,2,1,0:T(8,128)S(1)} add(f32[4,4,64,128]{3,2,1,0:T(8,128)} %get-tuple-element.11, f32[4,4,64,128]{3,2,1,0:T(8,128)S(1)} %collective-permute-done) | non-fusion elementwise | flops 131072 | bytes 1572864 | tf_op jit(solution)/shard_map/add | solution.py:123
  22.0 12.9 %all_to_all.20 = f32[16,64,128]{2,1,0:T(8,128)S(1)} all-to-all(f32[16,64,128]{2,1,0:T(8,128)S(1)} %bitcast.35), channel_id=1, replica_groups=mesh['x'=4,'y'=4,'h'=4,'l'=4,'c'=2] {'x','y'}, dimensions={0} | all-to-all | bytes 1048576 | tf_op jit(solution)/shard_map/all_to_all | solution.py:107
  35.0 0.7 broadcast_in_dim.8
  35.6 13.6 %all-to-all-start.1 = ((f32[16,16,128]{2,1,0:T(8,128)}), f32[16,16,128]{2,1,0:T(8,128)S(1)}, u32[]{:S(2)}, u32[]{:S(2)}) async-start(f32[16,16,128]{2,1,0:T(8,128)} %bitcast.17), calls=%async_computation.1 | async-start | bytes 262144 | tf_op jit(solution)/shard_map/all_to_all | solution.py:107
  49.2 0.1 pad.2.clone
  49.3 11.9 %all-to-all-done.1 = f32[16,16,128]{2,1,0:T(8,128)S(1)} async-done(((f32[16,16,128]{2,1,0:T(8,128)}), f32[16,16,128]{2,1,0:T(8,128)S(1)}, u32[]{:S(2)}, u32[]{:S(2)}) %all-to-all-start.1) | async-done | bytes 131104 | tf_op jit(solution)/shard_map/all_to_all | solution.py:107
  61.3 0.1 maximum_maximum_fusion
  61.3 0.6 broadcast_in_dim.10
  61.9 7.1 %all-to-all-start.2 = ((f32[8,8,128]{2,1,0:T(8,128)}), f32[8,8,128]{2,1,0:T(8,128)S(1)}, u32[]{:S(2)}, u32[]{:S(2)}) async-start(f32[8,8,128]{2,1,0:T(8,128)} %broadcast_in_dim.10), calls=%async_computation.2 | async-start | bytes 65536 | tf_op jit(solution)/shard_map/all_to_all | solution.py:107
  69.0 0.0 copy-done.1
  69.0 0.1 reduce_sum.54
  69.1 4.6 %all-to-all-done.2 = f32[8,8,128]{2,1,0:T(8,128)S(1)} async-done(((f32[8,8,128]{2,1,0:T(8,128)}), f32[8,8,128]{2,1,0:T(8,128)S(1)}, u32[]{:S(2)}, u32[]{:S(2)}) %all-to-all-start.2) | async-done | bytes 32800 | tf_op jit(solution)/shard_map/all_to_all | solution.py:107
  73.8 0.6 broadcast_in_dim.11
  74.4 3.8 %all-to-all-start.3 = ((f32[16,2,128]{2,1,0:T(2,128)}), f32[16,2,128]{2,1,0:T(2,128)S(1)}, u32[]{:S(2)}, u32[]{:S(2)}) async-start(f32[16,2,128]{2,1,0:T(2,128)} %broadcast_in_dim.11), calls=%async_computation.3 | async-start | bytes 32768 | tf_op jit(solution)/shard_map/all_to_all | solution.py:107
  78.2 6.7 %all-to-all-done.3 = f32[16,2,128]{2,1,0:T(2,128)S(1)} async-done(((f32[16,2,128]{2,1,0:T(2,128)}), f32[16,2,128]{2,1,0:T(2,128)S(1)}, u32[]{:S(2)}, u32[]{:S(2)}) %all-to-all-start.3) | async-done | bytes 16416 | tf_op jit(solution)/shard_map/all_to_all | solution.py:107
  84.9 0.1 reduce_sum.59
  85.1 0.0 copy-done
  85.1 0.7 multiply_subtract_fusion
  (14 shorter events, 0.2 us)
Async XLA Ops:
  10.3 58.8 %copy-start.1 = (f32[2,8,128]{2,1,0:T(8,128)S(1)}, f32[2,8,128]{2,1,0:T(8,128)}, u32[]{:S(2)}) copy-start(f32[2,8,128]{2,1,0:T(8,128)} %get-tuple-element.10) | copy-start | bytes 24580
  10.3 74.8 %copy-start = (f32[16,128]{1,0:T(8,128)S(1)}, f32[16,128]{1,0:T(8,128)}, u32[]{:S(2)}) copy-start(f32[16,128]{1,0:T(8,128)} %get-tuple-element.9) | copy-start | bytes 24580
  10.3 10.6 %collective-permute-start = (f32[4,4,64,128]{3,2,1,0:T(8,128)}, f32[4,4,64,128]{3,2,1,0:T(8,128)S(1)}, u32[]{:S(2)}, u32[]{:S(2)}) collective-permute-start(f32[4,4,64,128]{3,2,1,0:T(8,128)} %get-tuple-element.12), channel_id=1, source_target_pairs={{0,1},{1,0},{2,3},{3,2},{4,5},{5,4},{6,7},{7,6},{8,9},{9,8},{10,11... | collective-permute-start | bytes 1572872 | tf_op jit(solution)/shard_map/ppermute | solution.py:123
  35.6 25.6 %all-to-all-start.1 = ((f32[16,16,128]{2,1,0:T(8,128)}), f32[16,16,128]{2,1,0:T(8,128)S(1)}, u32[]{:S(2)}, u32[]{:S(2)}) async-start(f32[16,16,128]{2,1,0:T(8,128)} %bitcast.17), calls=%async_computation.1 | async-start | bytes 262144 | tf_op jit(solution)/shard_map/all_to_all | solution.py:107
  61.9 11.8 %all-to-all-start.2 = ((f32[8,8,128]{2,1,0:T(8,128)}), f32[8,8,128]{2,1,0:T(8,128)S(1)}, u32[]{:S(2)}, u32[]{:S(2)}) async-start(f32[8,8,128]{2,1,0:T(8,128)} %broadcast_in_dim.10), calls=%async_computation.2 | async-start | bytes 65536 | tf_op jit(solution)/shard_map/all_to_all | solution.py:107
  74.4 10.6 %all-to-all-start.3 = ((f32[16,2,128]{2,1,0:T(2,128)}), f32[16,2,128]{2,1,0:T(2,128)S(1)}, u32[]{:S(2)}, u32[]{:S(2)}) async-start(f32[16,2,128]{2,1,0:T(2,128)} %broadcast_in_dim.11), calls=%async_computation.3 | async-start | bytes 32768 | tf_op jit(solution)/shard_map/all_to_all | solution.py:107

commit v4 on v3

--- a/solution.py
+++ b/solution.py
@@ -16,18 +16,18 @@
 
 
 def grads_kernel(
-    ny, nz, at_ref, low_ref, q_ref, d_ref, lse_ref, dot_ref,
+    ny, nz, core_ref, first_ref, low_ref, q_ref, d_ref, lse_ref, dot_ref,
     send_ref, own_ref, sq_ref, own_w_ref, w_ref,
 ):
     group = pl.program_id(0)
-    core = at_ref[0]
+    core = core_ref[0]
     heads = lse_ref.shape[0]
 
     @pl.when(group == 0)
     def _():
         w_ref[...] = low_ref[...].astype(F32)
         sq_ref[...] = jnp.zeros_like(sq_ref)
-        start = pl.multiple_of(at_ref[1] * 8, 8)
+        start = pl.multiple_of(first_ref[0] * 8, 8)
         own_w_ref[...] = w_ref[pl.ds(start, own_w_ref.shape[0]), :]
 
     sides = []
@@ -66,7 +66,7 @@
                 at += nz
 
 
-def local_grads(nx, ny, nz, own, place, weights, queries, grad_out, seq_lse, out_dot):
+def local_grads(nx, ny, nz, own, core, first, weights, queries, grad_out, seq_lse, out_dot):
     tok, cols = queries.shape
     heads = seq_lse.shape[0] // nx
     half = jax.ShapeDtypeStruct((nx, ny, nz * 4, HEAD), F32)
@@ -75,6 +75,7 @@
         functools.partial(grads_kernel, ny, nz),
         grid=(nx,),
         in_specs=[
+            pl.BlockSpec(memory_space=pltpu.SMEM),
             pl.BlockSpec(memory_space=pltpu.SMEM),
             pl.BlockSpec(weights.shape, lambda g: (0, 0)),
             pl.BlockSpec((tok, cols // nx), lambda g: (0, g)),
@@ -97,7 +98,7 @@
         scratch_shapes=[pltpu.VMEM(weights.shape, F32)],
         compiler_params=pltpu.CompilerParams(vmem_limit_bytes=60 * 2**20),
         name="prefix_grads",
-    )(place, weights, queries, grad_out, seq_lse, out_dot)
+    )(core.reshape(1), first.reshape(1), weights, queries, grad_out, seq_lse, out_dot)
 
 
 def make_body(nx, ny, nh, nl, nc):
@@ -117,28 +118,31 @@
         first = lax.axis_index(("y", "h", "l", "c")) * own
         weights = prefix.reshape(rows_all, 2, nx, part).transpose(0, 2, 1, 3).reshape(-1, part)
         send, mine, w_squares, own_weights = local_grads(
-            nx, ny, nz, own, jnp.stack([core, first]), weights,
+            nx, ny, nz, own, core, first, weights,
             queries[0], grad_out[0], seq_lse[0].T, out_dot[0].T,
         )
         half = mine + lax.ppermute(send, "c", [(i, (i + 1) % nc) for i in range(nc)])
+        weight_ms = w_squares.sum((1, 2)) / (rows_all * width)
+        at_h = lax.axis_index("h").astype(jnp.uint32)
+        at_yl = lax.axis_index(("y", "l")).astype(jnp.uint32)
+        half, weight_ms, own_weights, at_h, at_yl = lax.optimization_barrier(
+            (half, weight_ms, own_weights, at_h, at_yl)
+        )
         rows = 2 * own
         plane = exchange(half.reshape(nx * ny, nz * rows, part), ("x", "y")).sum(0)
         plane = plane.reshape(nh, nl, rows, part).transpose(1, 0, 2, 3)
         plane = jnp.broadcast_to(plane[None], (nh,) + plane.shape).reshape(nz, nh * rows, part)
         piece = exchange(plane, ("h", "l")).sum(0).reshape(nh, 2, own, part)
-        squares = (piece * piece).sum((0, 2))
-        piece = lax.dynamic_index_in_dim(piece, lax.axis_index("h"), 0, keepdims=False)
-        packed = jnp.concatenate(
-            [piece.reshape(rows, part), squares, jnp.zeros((8 - rows - 2, part), F32)], 0
-        )
-        packed = to_all(packed, ("x", "c"), nx * nc)
-        squares = packed[:, rows : rows + 2].sum(0)
-        packed = packed[:, :rows].reshape(nx, nc, 2, own, part)
-        own_grads = lax.dynamic_index_in_dim(packed, core, 1, keepdims=False)
-        grad_ms = to_all(squares, ("y", "l"), ny * nl).sum((0, 2)) / (rows_all * width)
-        weight_ms = w_squares.sum((1, 2)) / (rows_all * width)
+        squares = lax.all_gather((piece * piece).sum((0, 2)), "c").sum(0)
+        squares = squares.reshape(2, 2, part // 2).sum(1).reshape(1, part)
+        piece = lax.dynamic_index_in_dim(piece, at_h, 0, keepdims=False)
+        packed = jnp.concatenate([piece.reshape(rows, part), squares], 0).reshape(1, -1)
+        packed = to_all(packed, ("x", "y", "l"), nx * ny * nl)
+        grad_ms = packed[:, 0, rows * part :].reshape(-1, 2, part // 2).sum((0, 2)) / (rows_all * width)
+        packed = packed.reshape(nx, ny * nl, -1)
+        own_grads = lax.dynamic_index_in_dim(packed, at_yl, 1, keepdims=False)[:, : rows * part]
+        own_grads = own_grads.reshape(nx, 2, own, part).transpose(2, 1, 0, 3).reshape(own, 2, width)
         ratio = jnp.sqrt(weight_ms) / jnp.sqrt(grad_ms + 1e-06)
-        own_grads = own_grads.transpose(2, 1, 0, 3).reshape(own, 2, width)
         own_weights = own_weights.reshape(own, nx, 2, part).transpose(0, 2, 1, 3).reshape(own, 2, width)
         return own_weights - 0.5 * ratio[None, :, None] * own_grads
 

time: 86.2 us -> 82.1 us (0.952)
  blocking collectives: 12.9 us -> 59.1 us
  starting transfers between devices: 33.3 us -> 8.73 us
  waiting for transfers between devices: 25 us -> 0.91 us
  local copies, waits for them, and re-layouts: 2.02 us -> 0.43 us
    all_to_all x1 -> x3, blocking collectives: 12.9 us -> 53.8 us  [exchange(): return lax.all_to_all(block, axes, 0, 0, tiled=True)]
    all_to_all x3 -> x0, starting transfers between devices: 24.4 us -> none  [exchange(): return lax.all_to_all(block, axes, 0, 0, tiled=True)]
    all_to_all x3 -> x0, waiting for transfers between devices: 23.3 us -> none  [exchange(): return lax.all_to_all(block, axes, 0, 0, tiled=True)]
    all_gather x0 -> x1, blocking collectives: none -> 5.3 us  [body(): squares = lax.all_gather((piece * piece).sum((0, 2)), 'c').sum(0)]
    broadcast_in_dim x2 -> x1, local copies, waits for them, and re-layouts: 1.21 us -> 0.09 us  [to_all(): return exchange(jnp.broadcast_to(block[None], (count,) + block.shape), axes)]
  transfers between devices with their start and end apart: 4 -> 1, of which waited for: 4 -> 1; matrix products, arithmetic and copies ran while one was open for 0% -> 1% of each run, Pallas kernels for 0% -> 0%
where the time goes in v4:
time: 82.1 us; the launch traced here: 81.8 us
  blocking collectives  59.1 us (72%)
  Pallas kernels  9.6 us (12%)
  starting transfers between devices  8.73 us (11%)
  other arithmetic  2.92 us (4%)
  waiting for transfers between devices  0.91 us (1%)
    all_to_all x3, blocking collectives, exchange(): return lax.all_to_all(block, axes, 0, 0, tiled=True)  53.8 us
    pallas_call x1, Pallas kernels, local_grads(): pl.pallas_call(functools.partial(grads_kernel, ny, nz), grid=(nx,), in_sp...  9.6 us
    ppermute x1, starting transfers between devices, body(): lax.ppermute(send, 'c', [(i, (i + 1) % nc) for i in range(nc)])  8.73 us
    all_gather x1, blocking collectives, body(): squares = lax.all_gather((piece * piece).sum((0, 2)), 'c').sum(0)  5.3 us
  transfers between devices with their start and end apart: 1, of which 1 were waited for; matrix products, arithmetic and copies ran while one was open for 1% of the time, Pallas kernels for 0%

profile of v4, /device:TPU:1, one launch (start us, length us, event | category | flops | bytes accessed | tf_op | source)
XLA Modules:
  0.0 81.8 jit_solution(10034584507972189008)
XLA Ops:
  0.0 9.6 %prefix_grads.1 = (f32[4,4,64,128]{3,2,1,0:T(8,128)}, f32[4,4,64,128]{3,2,1,0:T(8,128)}, f32[2,8,128]{2,1,0:T(8,128)}, f32[16,128]{1,0:T(8,128)}) custom-call(s32[1]{0:T(128)} %bitcast.core_ref, s32[1]{0:T(128)} %bitcast.1.first_ref, bf16[2048,128]{1,0:T(8,128)(2,1)} %bitcast.43, bf16[128,8192]{1,0:T(8,128)(2,1)} %bitcast.40, bf16[128,8192]{1,0:T(8,128)(2,1)} %bitcast.41, ...), custom_call_target="tpu_custom_call" | custom-call | tf_op jit(solution)/shard_map/prefix_grads/pallas_call | solution.py:74
  9.6 8.7 %collective-permute-start = (f32[4,4,64,128]{3,2,1,0:T(8,128)}, f32[4,4,64,128]{3,2,1,0:T(8,128)S(1)}, u32[]{:S(2)}, u32[]{:S(2)}) collective-permute-start(f32[4,4,64,128]{3,2,1,0:T(8,128)} %get-tuple-element.15), channel_id=1, source_target_pairs={{0,1},{1,0},{2,3},{3,2},{4,5},{5,4},{6,7},{7,6},{8,9},{9,8},{10,11... | collective-permute-start | bytes 1572872 | tf_op jit(solution)/shard_map/ppermute | solution.py:124
  18.4 0.8 reduce_sum.70
  19.2 0.9 %collective-permute-done = f32[4,4,64,128]{3,2,1,0:T(8,128)S(1)} collective-permute-done((f32[4,4,64,128]{3,2,1,0:T(8,128)}, f32[4,4,64,128]{3,2,1,0:T(8,128)S(1)}, u32[]{:S(2)}, u32[]{:S(2)}) %collective-permute-start) | collective-permute-done | bytes 524320 | tf_op jit(solution)/shard_map/ppermute | solution.py:124
  20.1 0.0 copy-start
  20.1 1.1 %add.21 = f32[4,4,64,128]{3,2,1,0:T(8,128)S(1)} add(f32[4,4,64,128]{3,2,1,0:T(8,128)} %get-tuple-element.14, f32[4,4,64,128]{3,2,1,0:T(8,128)S(1)} %collective-permute-done) | non-fusion elementwise | flops 131072 | bytes 1572864 | tf_op jit(solution)/shard_map/add | solution.py:124
  21.2 12.9 %all_to_all.15 = f32[16,64,128]{2,1,0:T(8,128)S(1)} all-to-all(f32[16,64,128]{2,1,0:T(8,128)S(1)} %bitcast.39), channel_id=1, replica_groups=mesh['x'=4,'y'=4,'h'=4,'l'=4,'c'=2] {'x','y'}, dimensions={0} | all-to-all | bytes 1048576 | tf_op jit(solution)/shard_map/all_to_all | solution.py:108
  34.1 25.4 %all_to_all.16 = f32[16,16,128]{2,1,0:T(8,128)S(1)} all-to-all(f32[16,16,128]{2,1,0:T(8,128)S(1)} %bitcast.42), channel_id=1, replica_groups=mesh['x'=4,'y'=4,'h'=4,'l'=4,'c'=2] {'h','l'}, dimensions={0} | all-to-all | bytes 262144 | tf_op jit(solution)/shard_map/all_to_all | solution.py:108
  59.6 5.3 %all-gather.1 = f32[2,2,128]{2,1,0:T(2,128)S(1)} all-gather(f32[1,2,128]{2,1,0:T(2,128)S(1)} %bitcast.54), channel_id=2, replica_groups=mesh['x'=4,'y'=4,'h'=4,'l'=4,'c'=2] {'c'}, dimensions={0}, use_global_device_ids=true | all-gather | bytes 3072 | tf_op jit(solution)/shard_map/all_gather | solution.py:136
  64.9 0.1 reshape.67
  65.0 0.1 reshape.68
  65.1 0.1 broadcast_in_dim.16
  65.2 15.5 %all_to_all.17 = f32[64,1,640]{2,1,0:T(1,128)S(1)} all-to-all(f32[64,1,640]{2,1,0:T(1,128)S(1)} %broadcast_in_dim.16), channel_id=1, replica_groups=mesh['x'=4,'y'=4,'h'=4,'l'=4,'c'=2] {'x','y','l'}, dimensions={0} | all-to-all | bytes 327680 | tf_op jit(solution)/shard_map/all_to_all | solution.py:108
  80.8 0.1 slice_reduce_fusion
  80.9 0.1 reduce_sum.77
  81.0 0.1 reduce_sum.78
  81.1 0.0 copy-done
  81.1 0.7 fusion
  (16 shorter events, 0.2 us)
Async XLA Ops:
  9.6 10.5 %collective-permute-start = (f32[4,4,64,128]{3,2,1,0:T(8,128)}, f32[4,4,64,128]{3,2,1,0:T(8,128)S(1)}, u32[]{:S(2)}, u32[]{:S(2)}) collective-permute-start(f32[4,4,64,128]{3,2,1,0:T(8,128)} %get-tuple-element.15), channel_id=1, source_target_pairs={{0,1},{1,0},{2,3},{3,2},{4,5},{5,4},{6,7},{7,6},{8,9},{9,8},{10,11... | collective-permute-start | bytes 1572872 | tf_op jit(solution)/shard_map/ppermute | solution.py:124
  20.1 61.1 %copy-start = (f32[16,128]{1,0:T(8,128)S(1)}, f32[16,128]{1,0:T(8,128)}, u32[]{:S(2)}) copy-start(f32[16,128]{1,0:T(8,128)} %get-tuple-element.18) | copy-start | bytes 24580

commit v5 on v4

v5 whole, which is shorter than its diff:
```python
import functools

import jax
import jax.numpy as jnp
from jax import lax
from jax.experimental import pallas as pl
from jax.experimental.pallas import tpu as pltpu
from jax.sharding import Mesh, PartitionSpec as P

HEAD = 128
SCALE = HEAD ** (-0.5)
LOG2E = 1.4426950408889634
NT = (((1,), (1,)), ((), ()))
NN = (((1,), (0,)), ((), ()))
F32 = jnp.float32


def grads_kernel(
    ny, nz, core_ref, first_ref, low_hbm, q_hbm, d_hbm, lse_hbm, dot_hbm,
    send_ref, own_ref, sq_ref, own_w_ref,
    low_ref, q_ref, d_ref, lse_ref, dot_ref, w_ref, low_sem, row_sem, q_sem, d_sem,
):
    core = core_ref[0]
    groups, _, cols = q_ref.shape
    heads = cols // HEAD
    prefix_copy = pltpu.make_async_copy(low_hbm, low_ref, low_sem)
    row_copies = [
        pltpu.make_async_copy(lse_hbm, lse_ref, row_sem.at[0]),
        pltpu.make_async_copy(dot_hbm, dot_ref, row_sem.at[1]),
    ]

    def copies(g):
        span = pl.ds(g * cols, cols)
        return [
            pltpu.make_async_copy(q_hbm.at[:, span], q_ref.at[g], q_sem.at[g]),
            pltpu.make_async_copy(d_hbm.at[:, span], d_ref.at[g], d_sem.at[g]),
        ]

    prefix_copy.start()
    for copy in copies(0) + row_copies:
        copy.start()
    prefix_copy.wait()
    w_ref[...] = low_ref[...].astype(F32)
    start = pl.multiple_of(first_ref[0] * 8, 8)
    own_w_ref[...] = w_ref[pl.ds(start, own_w_ref.shape[0]), :]

    sides = []
    total = [jnp.zeros((8, HEAD), F32)] * 2
    for g in range(groups):
        for kv in range(2):
            rows = []
            for half in (1 - core, core):
                for y in range(ny):
                    for r in range(2):
                        first = y * nz * 32 + half * 16 + r * 8 + g * 2 + kv
                        block = w_ref[pl.ds(first, nz, stride=32), :]
                        total[kv] += (block * block).reshape(nz // 8, 8, HEAD).sum(0)
                        rows.append(block)
            sides.append(jnp.concatenate(rows, 0).astype(jnp.bfloat16))
    for kv in range(2):
        sq_ref[kv] = total[kv]
    for copy in row_copies:
        copy.wait()

    def rows_of(ref, g):
        return jnp.concatenate([ref[g, :, h * HEAD : (h + 1) * HEAD] for h in range(heads)], 0)

    def line_of(ref, g):
        return jnp.concatenate([ref[g * heads + h : g * heads + h + 1, :] for h in range(heads)], 1)

    def products(g):
        for copy in copies(g):
            copy.wait()
        if g + 1 < groups:
            for copy in copies(g + 1):
                copy.start()
        scores = lax.dot_general(sides[2 * g], rows_of(q_ref, g), NT, preferred_element_type=F32)
        dprobs = lax.dot_general(sides[2 * g + 1], rows_of(d_ref, g), NT, preferred_element_type=F32)
        return scores, dprobs

    def weights_of(g, scores, dprobs):
        lse = line_of(lse_ref, g) * LOG2E
        top = jnp.maximum(jnp.max(scores, axis=0, keepdims=True) * (SCALE * LOG2E), lse)
        probs = jnp.exp2(scores * (SCALE * LOG2E) - top)
        probs = probs * (1.0 / (jnp.sum(probs, axis=0, keepdims=True) + jnp.exp2(lse - top)))
        dscores = probs * (dprobs - line_of(dot_ref, g))
        return probs.astype(jnp.bfloat16), dscores.astype(jnp.bfloat16)

    def finish(g, probs, dscores):
        grad_v = lax.dot_general(probs, rows_of(d_ref, g), NN, preferred_element_type=F32)
        grad_k = lax.dot_general(dscores, rows_of(q_ref, g), NN, preferred_element_type=F32) * SCALE
        at = 0
        for ref in (send_ref, own_ref):
            for y in range(ny):
                for r in range(2):
                    ref[g, y, pl.ds(r, nz, stride=4), :] = grad_k[at : at + nz]
                    ref[g, y, pl.ds(2 + r, nz, stride=4), :] = grad_v[at : at + nz]
                    at += nz

    for g in range(groups - 1):
        finish(g, *weights_of(g, *products(g)))
    held = weights_of(groups - 1, *products(groups - 1))
    finish(groups - 1, *held)


def local_grads(nx, ny, nz, own, core, first, weights, queries, grad_out, seq_lse, out_dot):
    tok, cols = queries.shape
    half = jax.ShapeDtypeStruct((nx, ny, nz * 4, HEAD), F32)
    vmem = pl.BlockSpec(memory_space=pltpu.VMEM)
    smem = pl.BlockSpec(memory_space=pltpu.SMEM)
    hbm = pl.BlockSpec(memory_space=pltpu.HBM)
    operands = [weights, queries, grad_out, seq_lse, out_dot]
    operands = [pltpu.with_memory_space_constraint(x, pltpu.HBM) for x in operands]
    return pl.pallas_call(
        functools.partial(grads_kernel, ny, nz),
        in_specs=[smem, smem] + [hbm] * 5,
        out_specs=[vmem] * 4,
        out_shape=[half, half, jax.ShapeDtypeStruct((2, 8, HEAD), F32), jax.ShapeDtypeStruct((own * 8, HEAD), F32)],
        scratch_shapes=[
            pltpu.VMEM(weights.shape, weights.dtype),
            pltpu.VMEM((nx, tok, cols // nx), queries.dtype),
            pltpu.VMEM((nx, tok, cols // nx), grad_out.dtype),
            pltpu.VMEM(seq_lse.shape, F32),
            pltpu.VMEM(out_dot.shape, F32),
            pltpu.VMEM(weights.shape, F32),
            pltpu.SemaphoreType.DMA,
            pltpu.SemaphoreType.DMA((2,)),
            pltpu.SemaphoreType.DMA((nx,)),
            pltpu.SemaphoreType.DMA((nx,)),
        ],
        compiler_params=pltpu.CompilerParams(vmem_limit_bytes=40 * 2**20),
        name="prefix_grads",
    )(core.reshape(1), first.reshape(1), *operands)


def make_body(nx, ny, nh, nl, nc):
    nz = nh * nl

    def exchange(block, axes):
        return lax.all_to_all(block, axes, 0, 0, tiled=True)

    def to_all(block, axes, count):
        return exchange(jnp.broadcast_to(block[None], (count,) + block.shape), axes)

    def body(queries, grad_out, seq_lse, out_dot, prefix):
        rows_all, width = prefix.shape[0], prefix.shape[2]
        own = rows_all // (ny * nz * nc)
        part = width // nx
        core = lax.axis_index("c")
        first = lax.axis_index(("y", "h", "l", "c")) * own
        weights = prefix.reshape(rows_all, 2, nx, part).transpose(0, 2, 1, 3).reshape(-1, part)
        send, mine, w_squares, own_weights = local_grads(
            nx, ny, nz, own, core, first, weights,
            queries[0], grad_out[0], seq_lse[0].T, out_dot[0].T,
        )
        half = mine + lax.ppermute(send, "c", [(i, (i + 1) % nc) for i in range(nc)])
        weight_ms = w_squares.sum((1, 2)) / (rows_all * width)
        at_h = lax.axis_index("h").astype(jnp.uint32)
        at_yl = lax.axis_index(("y", "l")).astype(jnp.uint32)
        half, weight_ms, own_weights, at_h, at_yl = lax.optimization_barrier(
            (half, weight_ms, own_weights, at_h, at_yl)
        )
        rows = 2 * own
        plane = exchange(half.reshape(nx * ny, nz * rows, part), ("x", "y")).sum(0)
        plane = plane.reshape(nh, nl, rows, part).transpose(1, 0, 2, 3)
        plane = jnp.broadcast_to(plane[None], (nh,) + plane.shape).reshape(nz, nh * rows, part)
        piece = exchange(plane, ("h", "l")).sum(0).reshape(nh, 2, own, part)
        squares = lax.all_gather((piece * piece).sum((0, 2)), "c").sum(0)
        squares = squares.reshape(2, 2, part // 2).sum(1).reshape(1, part)
        piece = lax.dynamic_index_in_dim(piece, at_h, 0, keepdims=False)
        packed = jnp.concatenate([piece.reshape(rows, part), squares], 0).reshape(1, -1)
        packed = to_all(packed, ("x", "y", "l"), nx * ny * nl)
        grad_ms = packed[:, 0, rows * part :].reshape(-1, 2, part // 2).sum((0, 2)) / (rows_all * width)
        packed = packed.reshape(nx, ny * nl, -1)
        own_grads = lax.dynamic_index_in_dim(packed, at_yl, 1, keepdims=False)[:, : rows * part]
        own_grads = own_grads.reshape(nx, 2, own, part).transpose(2, 1, 0, 3).reshape(own, 2, width)
        ratio = jnp.sqrt(weight_ms) / jnp.sqrt(grad_ms + 1e-06)
        own_weights = own_weights.reshape(own, nx, 2, part).transpose(0, 2, 1, 3).reshape(own, 2, width)
        return own_weights - 0.5 * ratio[None, :, None] * own_grads

    return body


def solution(mesh):
    nx, ny, nh, nl, nc = mesh.shape["dp"], 4, 4, 4, 2
    grid = Mesh(mesh.devices.reshape(nx, ny, nh, nl, nc), ("x", "y", "h", "l", "c"))
    tokens = P("x", ("y", "h", "l", "c"), None)
    return jax.shard_map(
        make_body(nx, ny, nh, nl, nc),
        mesh=grid,
        in_specs=(tokens, tokens, tokens, tokens, P()),
        out_specs=P(("y", "h", "l", "c"), None, None),
        check_vma=False,
    )
```

time: 82.1 us -> 79.9 us (0.973)
  other arithmetic: 2.92 us -> 1.17 us
  Pallas kernels: 9.6 us -> 8.68 us
    add x1, other arithmetic: 1.11 us -> 0.06 us  [body(): mine + lax.ppermute(send, 'c', [(i, (i + 1) % nc) for i in range(nc)])]
    pallas_call x1, Pallas kernels: 9.6 us -> 8.68 us  [local_grads(): pl.pallas_call(functools.partial(grads_kernel, ny, nz), in_specs=[smem, s...]
  transfers between devices with their start and end apart: 1 -> 1, of which waited for: 1 -> 1; matrix products, arithmetic and copies ran while one was open for 1% -> 0% of each run, Pallas kernels for 0% -> 0%
where the time goes in v5:
time: 79.9 us; the launch traced here: 79.7 us
  blocking collectives  59.1 us (74%)
  starting transfers between devices  8.78 us (11%)
  Pallas kernels  8.68 us (11%)
  waiting for transfers between devices  1.4 us (2%)
  other arithmetic  1.17 us (1%)
    all_to_all x3, blocking collectives, exchange(): return lax.all_to_all(block, axes, 0, 0, tiled=True)  53.8 us
    ppermute x1, starting transfers between devices, body(): lax.ppermute(send, 'c', [(i, (i + 1) % nc) for i in range(nc)])  8.78 us
    pallas_call x1, Pallas kernels, local_grads(): pl.pallas_call(functools.partial(grads_kernel, ny, nz), in_specs=[smem, s...  8.68 us
    all_gather x1, blocking collectives, body(): squares = lax.all_gather((piece * piece).sum((0, 2)), 'c').sum(0)  5.3 us
  transfers between devices with their start and end apart: 1, of which 1 were waited for; matrix products, arithmetic and copies ran while one was open for 0% of the time, Pallas kernels for 0%

profile of v5, /device:TPU:1, one launch (start us, length us, event | category | flops | bytes accessed | tf_op | source)
XLA Modules:
  0.0 79.7 jit_solution(1778047623369574715)
XLA Ops:
  0.0 8.7 %prefix_grads.1 = (f32[4,4,64,128]{3,2,1,0:T(8,128)S(1)}, f32[4,4,64,128]{3,2,1,0:T(8,128)S(1)}, f32[2,8,128]{2,1,0:T(8,128)S(1)}, f32[16,128]{1,0:T(8,128)S(1)}) custom-call(s32[1]{0:T(128)} %bitcast.core_ref, s32[1]{0:T(128)} %bitcast.1.first_ref, bf16[2048,128]{1,0:T(8,128)(2,1)} %bitcast.44, bf16[128,8192]{1,0:T(8,128)(2,1)} %bitcast.41, ...), custom_call_target="tpu_custom_call" | custom-call | tf_op jit(solution)/shard_map/prefix_grads/pallas_call | solution.py:114
  8.7 8.8 %collective-permute-start = (f32[4,4,64,128]{3,2,1,0:T(8,128)S(1)}, f32[4,4,64,128]{3,2,1,0:T(8,128)S(1)}, u32[]{:S(2)}, u32[]{:S(2)}) collective-permute-start(f32[4,4,64,128]{3,2,1,0:T(8,128)S(1)} %get-tuple-element.15), channel_id=1, source_target_pairs={{0,1},{1,0},{2,3},{3,2},{4,5},{5,4},{6,7},{7,6},{8,9},{9,8},{10,11... | collective-permute-start | bytes 1572872 | tf_op jit(solution)/shard_map/ppermute | solution.py:156
  17.5 0.1 reduce_sum.70
  17.6 1.4 %collective-permute-done = f32[4,4,64,128]{3,2,1,0:T(8,128)S(1)} collective-permute-done((f32[4,4,64,128]{3,2,1,0:T(8,128)S(1)}, f32[4,4,64,128]{3,2,1,0:T(8,128)S(1)}, u32[]{:S(2)}, u32[]{:S(2)}) %collective-permute-start) | collective-permute-done | bytes 524320 | tf_op jit(solution)/shard_map/ppermute | solution.py:156
  19.0 0.1 add.21
  19.1 12.9 %all_to_all.15 = f32[16,64,128]{2,1,0:T(8,128)S(1)} all-to-all(f32[16,64,128]{2,1,0:T(8,128)S(1)} %bitcast.40), channel_id=1, replica_groups=mesh['x'=4,'y'=4,'h'=4,'l'=4,'c'=2] {'x','y'}, dimensions={0} | all-to-all | bytes 1048576 | tf_op jit(solution)/shard_map/all_to_all | solution.py:140
  32.0 25.4 %all_to_all.16 = f32[16,16,128]{2,1,0:T(8,128)S(1)} all-to-all(f32[16,16,128]{2,1,0:T(8,128)S(1)} %bitcast.43), channel_id=1, replica_groups=mesh['x'=4,'y'=4,'h'=4,'l'=4,'c'=2] {'h','l'}, dimensions={0} | all-to-all | bytes 262144 | tf_op jit(solution)/shard_map/all_to_all | solution.py:140
  57.4 5.3 %all-gather.1 = f32[2,2,128]{2,1,0:T(2,128)S(1)} all-gather(f32[1,2,128]{2,1,0:T(2,128)S(1)} %bitcast.54), channel_id=2, replica_groups=mesh['x'=4,'y'=4,'h'=4,'l'=4,'c'=2] {'c'}, dimensions={0}, use_global_device_ids=true | all-gather | bytes 3072 | tf_op jit(solution)/shard_map/all_gather | solution.py:168
  62.8 0.1 reshape.67
  62.9 0.1 reshape.68
  63.0 0.1 broadcast_in_dim.16
  63.1 15.5 %all_to_all.17 = f32[64,1,640]{2,1,0:T(1,128)S(1)} all-to-all(f32[64,1,640]{2,1,0:T(1,128)S(1)} %broadcast_in_dim.16), channel_id=1, replica_groups=mesh['x'=4,'y'=4,'h'=4,'l'=4,'c'=2] {'x','y','l'}, dimensions={0} | all-to-all | bytes 327680 | tf_op jit(solution)/shard_map/all_to_all | solution.py:140
  78.7 0.1 slice_reduce_fusion
  78.8 0.1 reduce_sum.77
  78.8 0.1 reduce_sum.78
  79.0 0.7 fusion
  (16 shorter events, 0.2 us)
Async XLA Ops:
  8.7 10.3 %collective-permute-start = (f32[4,4,64,128]{3,2,1,0:T(8,128)S(1)}, f32[4,4,64,128]{3,2,1,0:T(8,128)S(1)}, u32[]{:S(2)}, u32[]{:S(2)}) collective-permute-start(f32[4,4,64,128]{3,2,1,0:T(8,128)S(1)} %get-tuple-element.15), channel_id=1, source_target_pairs={{0,1},{1,0},{2,3},{3,2},{4,5},{5,4},{6,7},{7,6},{8,9},{9,8},{10,11... | collective-permute-start | bytes 1572872 | tf_op jit(solution)/shard_map/ppermute | solution.py:156

commit v6 on v5

--- a/solution.py
+++ b/solution.py
@@ -44,49 +44,34 @@
     start = pl.multiple_of(first_ref[0] * 8, 8)
     own_w_ref[...] = w_ref[pl.ds(start, own_w_ref.shape[0]), :]
 
-    sides = []
-    total = [jnp.zeros((8, HEAD), F32)] * 2
-    for g in range(groups):
-        for kv in range(2):
-            rows = []
-            for half in (1 - core, core):
-                for y in range(ny):
-                    for r in range(2):
-                        first = y * nz * 32 + half * 16 + r * 8 + g * 2 + kv
-                        block = w_ref[pl.ds(first, nz, stride=32), :]
-                        total[kv] += (block * block).reshape(nz // 8, 8, HEAD).sum(0)
-                        rows.append(block)
-            sides.append(jnp.concatenate(rows, 0).astype(jnp.bfloat16))
-    for kv in range(2):
-        sq_ref[kv] = total[kv]
-    for copy in row_copies:
-        copy.wait()
+    def gather(g, kv):
+        rows = []
+        for half in (1 - core, core):
+            for y in range(ny):
+                for r in range(2):
+                    first = y * nz * 32 + half * 16 + r * 8 + g * 2 + kv
+                    rows.append(w_ref[pl.ds(first, nz, stride=32), :])
+        return jnp.concatenate(rows, 0)
 
     def rows_of(ref, g):
         return jnp.concatenate([ref[g, :, h * HEAD : (h + 1) * HEAD] for h in range(heads)], 0)
 
     def line_of(ref, g):
-        return jnp.concatenate([ref[g * heads + h : g * heads + h + 1, :] for h in range(heads)], 1)
-
-    def products(g):
-        for copy in copies(g):
-            copy.wait()
-        if g + 1 < groups:
-            for copy in copies(g + 1):
-                copy.start()
-        scores = lax.dot_general(sides[2 * g], rows_of(q_ref, g), NT, preferred_element_type=F32)
-        dprobs = lax.dot_general(sides[2 * g + 1], rows_of(d_ref, g), NT, preferred_element_type=F32)
-        return scores, dprobs
-
-    def weights_of(g, scores, dprobs):
+        lines = ref[pl.ds(g * heads, heads), :]
+        return jnp.concatenate([lines[h : h + 1, :] for h in range(heads)], 1)
+
+    def group(g, keys, values, stable):
+        scores = lax.dot_general(keys, rows_of(q_ref, g), NT, preferred_element_type=F32)
+        dprobs = lax.dot_general(values, rows_of(d_ref, g), NT, preferred_element_type=F32)
         lse = line_of(lse_ref, g) * LOG2E
-        top = jnp.maximum(jnp.max(scores, axis=0, keepdims=True) * (SCALE * LOG2E), lse)
+        top = lse
+        if stable:
+            top = jnp.maximum(jnp.max(scores, axis=0, keepdims=True) * (SCALE * LOG2E), lse)
         probs = jnp.exp2(scores * (SCALE * LOG2E) - top)
-        probs = probs * (1.0 / (jnp.sum(probs, axis=0, keepdims=True) + jnp.exp2(lse - top)))
-        dscores = probs * (dprobs - line_of(dot_ref, g))
-        return probs.astype(jnp.bfloat16), dscores.astype(jnp.bfloat16)
-
-    def finish(g, probs, dscores):
+        total = jnp.sum(probs, axis=0, keepdims=True)
+        probs = probs * (1.0 / (total + (jnp.exp2(lse - top) if stable else 1.0)))
+        dscores = (probs * (dprobs - line_of(dot_ref, g))).astype(jnp.bfloat16)
+        probs = probs.astype(jnp.bfloat16)
         grad_v = lax.dot_general(probs, rows_of(d_ref, g), NN, preferred_element_type=F32)
         grad_k = lax.dot_general(dscores, rows_of(q_ref, g), NN, preferred_element_type=F32) * SCALE
         at = 0
@@ -96,11 +81,32 @@
                     ref[g, y, pl.ds(r, nz, stride=4), :] = grad_k[at : at + nz]
                     ref[g, y, pl.ds(2 + r, nz, stride=4), :] = grad_v[at : at + nz]
                     at += nz
-
-    for g in range(groups - 1):
-        finish(g, *weights_of(g, *products(g)))
-    held = weights_of(groups - 1, *products(groups - 1))
-    finish(groups - 1, *held)
+        return total
+
+    sides = []
+    for kv in range(2):
+        sides.append([gather(g, kv) for g in range(groups)])
+        sq_ref[kv] = sum((x * x).reshape(-1, 8, HEAD).sum(0) for x in sides[kv])
+    for copy in row_copies:
+        copy.wait()
+    peak = None
+    for g in range(groups):
+        for copy in copies(g):
+            copy.wait()
+        if g + 1 < groups:
+            for copy in copies(g + 1):
+                copy.start()
+        keys, values = (sides[kv][g].astype(jnp.bfloat16) for kv in range(2))
+        total = group(g, keys, values, False)
+        peak = total if peak is None else jnp.maximum(peak, total)
+
+    @pl.when(jnp.max(peak) > 2.0**100)
+    def _():
+        def again(g, carry):
+            group(g, gather(g, 0).astype(jnp.bfloat16), gather(g, 1).astype(jnp.bfloat16), True)
+            return carry
+
+        lax.fori_loop(0, groups, again, 0)
 
 
 def local_grads(nx, ny, nz, own, core, first, weights, queries, grad_out, seq_lse, out_dot):

time: 79.9 us -> 85.5 us (1.070)
  Pallas kernels: 8.68 us -> 14.3 us
    pallas_call x1, Pallas kernels: 8.68 us -> 14.3 us  [local_grads(): pl.pallas_call(functools.partial(grads_kernel, ny, nz), in_specs=[smem, s...]
where the time goes in v6:
time: 85.5 us; the launch traced here: 85.3 us
  blocking collectives  59.1 us (69%)
  Pallas kernels  14.3 us (17%)
  starting transfers between devices  8.74 us (10%)
  waiting for transfers between devices  1.4 us (2%)
  other arithmetic  1.17 us (1%)
    all_to_all x3, blocking collectives, exchange(): return lax.all_to_all(block, axes, 0, 0, tiled=True)  53.8 us
    pallas_call x1, Pallas kernels, local_grads(): pl.pallas_call(functools.partial(grads_kernel, ny, nz), in_specs=[smem, s...  14.3 us
    ppermute x1, starting transfers between devices, body(): lax.ppermute(send, 'c', [(i, (i + 1) % nc) for i in range(nc)])  8.74 us
    all_gather x1, blocking collectives, body(): squares = lax.all_gather((piece * piece).sum((0, 2)), 'c').sum(0)  5.3 us
  transfers between devices with their start and end apart: 1, of which 1 were waited for; matrix products, arithmetic and copies ran while one was open for 0% of the time, Pallas kernels for 0%

profile of v6, /device:TPU:1, one launch (start us, length us, event | category | flops | bytes accessed | tf_op | source)
XLA Modules:
  0.0 85.3 jit_solution(11126912152695938508)
XLA Ops:
  0.0 14.3 %prefix_grads.1 = (f32[4,4,64,128]{3,2,1,0:T(8,128)S(1)}, f32[4,4,64,128]{3,2,1,0:T(8,128)S(1)}, f32[2,8,128]{2,1,0:T(8,128)S(1)}, f32[16,128]{1,0:T(8,128)S(1)}) custom-call(s32[1]{0:T(128)} %bitcast.core_ref, s32[1]{0:T(128)} %bitcast.1.first_ref, bf16[2048,128]{1,0:T(8,128)(2,1)} %bitcast.44, bf16[128,8192]{1,0:T(8,128)(2,1)} %bitcast.41, ...), custom_call_target="tpu_custom_call" | custom-call | tf_op jit(solution)/shard_map/prefix_grads/pallas_call | solution.py:120
  14.3 8.7 %collective-permute-start = (f32[4,4,64,128]{3,2,1,0:T(8,128)S(1)}, f32[4,4,64,128]{3,2,1,0:T(8,128)S(1)}, u32[]{:S(2)}, u32[]{:S(2)}) collective-permute-start(f32[4,4,64,128]{3,2,1,0:T(8,128)S(1)} %get-tuple-element.15), channel_id=1, source_target_pairs={{0,1},{1,0},{2,3},{3,2},{4,5},{5,4},{6,7},{7,6},{8,9},{9,8},{10,11... | collective-permute-start | bytes 1572872 | tf_op jit(solution)/shard_map/ppermute | solution.py:162
  23.1 0.1 reduce_sum.70
  23.2 1.4 %collective-permute-done = f32[4,4,64,128]{3,2,1,0:T(8,128)S(1)} collective-permute-done((f32[4,4,64,128]{3,2,1,0:T(8,128)S(1)}, f32[4,4,64,128]{3,2,1,0:T(8,128)S(1)}, u32[]{:S(2)}, u32[]{:S(2)}) %collective-permute-start) | collective-permute-done | bytes 524320 | tf_op jit(solution)/shard_map/ppermute | solution.py:162
  24.6 0.1 add.21
  24.7 12.9 %all_to_all.15 = f32[16,64,128]{2,1,0:T(8,128)S(1)} all-to-all(f32[16,64,128]{2,1,0:T(8,128)S(1)} %bitcast.40), channel_id=1, replica_groups=mesh['x'=4,'y'=4,'h'=4,'l'=4,'c'=2] {'x','y'}, dimensions={0} | all-to-all | bytes 1048576 | tf_op jit(solution)/shard_map/all_to_all | solution.py:146
  37.6 25.4 %all_to_all.16 = f32[16,16,128]{2,1,0:T(8,128)S(1)} all-to-all(f32[16,16,128]{2,1,0:T(8,128)S(1)} %bitcast.43), channel_id=1, replica_groups=mesh['x'=4,'y'=4,'h'=4,'l'=4,'c'=2] {'h','l'}, dimensions={0} | all-to-all | bytes 262144 | tf_op jit(solution)/shard_map/all_to_all | solution.py:146
  63.1 5.3 %all-gather.1 = f32[2,2,128]{2,1,0:T(2,128)S(1)} all-gather(f32[1,2,128]{2,1,0:T(2,128)S(1)} %bitcast.54), channel_id=2, replica_groups=mesh['x'=4,'y'=4,'h'=4,'l'=4,'c'=2] {'c'}, dimensions={0}, use_global_device_ids=true | all-gather | bytes 3072 | tf_op jit(solution)/shard_map/all_gather | solution.py:174
  68.4 0.1 reshape.67
  68.5 0.1 reshape.68
  68.6 0.1 broadcast_in_dim.16
  68.7 15.5 %all_to_all.17 = f32[64,1,640]{2,1,0:T(1,128)S(1)} all-to-all(f32[64,1,640]{2,1,0:T(1,128)S(1)} %broadcast_in_dim.16), channel_id=1, replica_groups=mesh['x'=4,'y'=4,'h'=4,'l'=4,'c'=2] {'x','y','l'}, dimensions={0} | all-to-all | bytes 327680 | tf_op jit(solution)/shard_map/all_to_all | solution.py:146
  84.3 0.1 slice_reduce_fusion
  84.4 0.1 reduce_sum.77
  84.5 0.1 reduce_sum.78
  84.6 0.7 fusion
  (16 shorter events, 0.2 us)
Async XLA Ops:
  14.3 10.3 %collective-permute-start = (f32[4,4,64,128]{3,2,1,0:T(8,128)S(1)}, f32[4,4,64,128]{3,2,1,0:T(8,128)S(1)}, u32[]{:S(2)}, u32[]{:S(2)}) collective-permute-start(f32[4,4,64,128]{3,2,1,0:T(8,128)S(1)} %get-tuple-element.15), channel_id=1, source_target_pairs={{0,1},{1,0},{2,3},{3,2},{4,5},{5,4},{6,7},{7,6},{8,9},{9,8},{10,11... | collective-permute-start | bytes 1572872 | tf_op jit(solution)/shard_map/ppermute | solution.py:162

commit v7 on v6

--- a/solution.py
+++ b/solution.py
@@ -162,24 +162,24 @@
         half = mine + lax.ppermute(send, "c", [(i, (i + 1) % nc) for i in range(nc)])
         weight_ms = w_squares.sum((1, 2)) / (rows_all * width)
         at_h = lax.axis_index("h").astype(jnp.uint32)
-        at_yl = lax.axis_index(("y", "l")).astype(jnp.uint32)
-        half, weight_ms, own_weights, at_h, at_yl = lax.optimization_barrier(
-            (half, weight_ms, own_weights, at_h, at_yl)
+        at_c = core.astype(jnp.uint32)
+        half, weight_ms, own_weights, at_h, at_c = lax.optimization_barrier(
+            (half, weight_ms, own_weights, at_h, at_c)
         )
         rows = 2 * own
         plane = exchange(half.reshape(nx * ny, nz * rows, part), ("x", "y")).sum(0)
         plane = plane.reshape(nh, nl, rows, part).transpose(1, 0, 2, 3)
         plane = jnp.broadcast_to(plane[None], (nh,) + plane.shape).reshape(nz, nh * rows, part)
         piece = exchange(plane, ("h", "l")).sum(0).reshape(nh, 2, own, part)
-        squares = lax.all_gather((piece * piece).sum((0, 2)), "c").sum(0)
-        squares = squares.reshape(2, 2, part // 2).sum(1).reshape(1, part)
-        piece = lax.dynamic_index_in_dim(piece, at_h, 0, keepdims=False)
-        packed = jnp.concatenate([piece.reshape(rows, part), squares], 0).reshape(1, -1)
-        packed = to_all(packed, ("x", "y", "l"), nx * ny * nl)
-        grad_ms = packed[:, 0, rows * part :].reshape(-1, 2, part // 2).sum((0, 2)) / (rows_all * width)
-        packed = packed.reshape(nx, ny * nl, -1)
-        own_grads = lax.dynamic_index_in_dim(packed, at_yl, 1, keepdims=False)[:, : rows * part]
-        own_grads = own_grads.reshape(nx, 2, own, part).transpose(2, 1, 0, 3).reshape(own, 2, width)
+        squares = (piece * piece).sum((0, 2))
+        piece = lax.dynamic_index_in_dim(piece, at_h, 0, keepdims=False).reshape(rows, part)
+        packed = to_all(jnp.concatenate([piece, squares, squares], 0), ("x", "c"), nx * nc)
+        squares = packed[:, rows : rows + 2].sum(0)
+        packed = packed[:, :rows].reshape(nx, nc, 2, own, part)
+        own_grads = lax.dynamic_index_in_dim(packed, at_c, 1, keepdims=False)
+        own_grads = own_grads.transpose(2, 1, 0, 3).reshape(own, 2, width)
+        own_grads, squares = lax.optimization_barrier((own_grads, squares))
+        grad_ms = to_all(squares, ("y", "l"), ny * nl).sum((0, 2)) / (rows_all * width)
         ratio = jnp.sqrt(weight_ms) / jnp.sqrt(grad_ms + 1e-06)
         own_weights = own_weights.reshape(own, nx, 2, part).transpose(0, 2, 1, 3).reshape(own, 2, width)
         return own_weights - 0.5 * ratio[None, :, None] * own_grads

time: 85.5 us -> 86 us (level)
    all_to_all x3 -> x4, blocking collectives: 53.8 us -> 59.9 us  [exchange(): return lax.all_to_all(block, axes, 0, 0, tiled=True)]
    all_gather x1 -> x0, blocking collectives: 5.3 us -> none  [body(): squares = lax.all_gather((piece * piece).sum((0, 2)), 'c').sum(0)]
where the time goes in v7:
time: 86 us; the launch traced here: 85.7 us
  blocking collectives  59.9 us (70%)
  Pallas kernels  14.3 us (17%)
  starting transfers between devices  8.74 us (10%)
  waiting for transfers between devices  1.41 us (2%)
  other arithmetic  1.09 us (1%)
    all_to_all x4, blocking collectives, exchange(): return lax.all_to_all(block, axes, 0, 0, tiled=True)  59.9 us
    pallas_call x1, Pallas kernels, local_grads(): pl.pallas_call(functools.partial(grads_kernel, ny, nz), in_specs=[smem, s...  14.3 us
    ppermute x1, starting transfers between devices, body(): lax.ppermute(send, 'c', [(i, (i + 1) % nc) for i in range(nc)])  8.74 us
  transfers between devices with their start and end apart: 1, of which 1 were waited for; matrix products, arithmetic and copies ran while one was open for 0% of the time, Pallas kernels for 0%

profile of v7, /device:TPU:1, one launch (start us, length us, event | category | flops | bytes accessed | tf_op | source)
XLA Modules:
  0.0 85.7 jit_solution(7074505827546915782)
XLA Ops:
  0.0 14.3 %prefix_grads.1 = (f32[4,4,64,128]{3,2,1,0:T(8,128)S(1)}, f32[4,4,64,128]{3,2,1,0:T(8,128)S(1)}, f32[2,8,128]{2,1,0:T(8,128)S(1)}, f32[16,128]{1,0:T(8,128)S(1)}) custom-call(s32[1]{0:T(128)} %bitcast.core_ref, s32[1]{0:T(128)} %bitcast.1.first_ref, bf16[2048,128]{1,0:T(8,128)(2,1)} %bitcast.38, bf16[128,8192]{1,0:T(8,128)(2,1)} %bitcast.35, ...), custom_call_target="tpu_custom_call" | custom-call | tf_op jit(solution)/shard_map/prefix_grads/pallas_call | solution.py:120
  14.3 8.7 %collective-permute-start = (f32[4,4,64,128]{3,2,1,0:T(8,128)S(1)}, f32[4,4,64,128]{3,2,1,0:T(8,128)S(1)}, u32[]{:S(2)}, u32[]{:S(2)}) collective-permute-start(f32[4,4,64,128]{3,2,1,0:T(8,128)S(1)} %get-tuple-element.17), channel_id=1, source_target_pairs={{0,1},{1,0},{2,3},{3,2},{4,5},{5,4},{6,7},{7,6},{8,9},{9,8},{10,11... | collective-permute-start | bytes 1572872 | tf_op jit(solution)/shard_map/ppermute | solution.py:162
  23.1 0.1 reduce_sum.54
  23.2 1.4 %collective-permute-done = f32[4,4,64,128]{3,2,1,0:T(8,128)S(1)} collective-permute-done((f32[4,4,64,128]{3,2,1,0:T(8,128)S(1)}, f32[4,4,64,128]{3,2,1,0:T(8,128)S(1)}, u32[]{:S(2)}, u32[]{:S(2)}) %collective-permute-start) | collective-permute-done | bytes 524320 | tf_op jit(solution)/shard_map/ppermute | solution.py:162
  24.6 0.1 add.18
  24.7 12.9 %all_to_all.20 = f32[16,64,128]{2,1,0:T(8,128)S(1)} all-to-all(f32[16,64,128]{2,1,0:T(8,128)S(1)} %bitcast.34), channel_id=1, replica_groups=mesh['x'=4,'y'=4,'h'=4,'l'=4,'c'=2] {'x','y'}, dimensions={0} | all-to-all | bytes 1048576 | tf_op jit(solution)/shard_map/all_to_all | solution.py:146
  37.6 25.4 %all_to_all.21 = f32[16,16,128]{2,1,0:T(8,128)S(1)} all-to-all(f32[16,16,128]{2,1,0:T(8,128)S(1)} %bitcast.37), channel_id=1, replica_groups=mesh['x'=4,'y'=4,'h'=4,'l'=4,'c'=2] {'h','l'}, dimensions={0} | all-to-all | bytes 262144 | tf_op jit(solution)/shard_map/all_to_all | solution.py:146
  63.1 11.2 %all_to_all.22 = f32[8,8,128]{2,1,0:T(8,128)S(1)} all-to-all(f32[8,8,128]{2,1,0:T(8,128)S(1)} %broadcast_in_dim.7), channel_id=1, replica_groups=mesh['x'=4,'y'=4,'h'=4,'l'=4,'c'=2] {'x','c'}, dimensions={0} | all-to-all | bytes 65536 | tf_op jit(solution)/shard_map/all_to_all | solution.py:146
  74.4 10.5 %all_to_all.23 = f32[16,2,128]{2,1,0:T(2,128)S(1)} all-to-all(f32[16,2,128]{2,1,0:T(2,128)S(1)} %broadcast_in_dim.8), channel_id=1, replica_groups=mesh['x'=4,'y'=4,'h'=4,'l'=4,'c'=2] {'y','l'}, dimensions={0} | all-to-all | bytes 32768 | tf_op jit(solution)/shard_map/all_to_all | solution.py:146
  84.9 0.1 reduce_sum.59
  85.0 0.7 multiply_subtract_fusion
  (18 shorter events, 0.2 us)
Async XLA Ops:
  14.3 10.3 %collective-permute-start = (f32[4,4,64,128]{3,2,1,0:T(8,128)S(1)}, f32[4,4,64,128]{3,2,1,0:T(8,128)S(1)}, u32[]{:S(2)}, u32[]{:S(2)}) collective-permute-start(f32[4,4,64,128]{3,2,1,0:T(8,128)S(1)} %get-tuple-element.17), channel_id=1, source_target_pairs={{0,1},{1,0},{2,3},{3,2},{4,5},{5,4},{6,7},{7,6},{8,9},{9,8},{10,11... | collective-permute-start | bytes 1572872 | tf_op jit(solution)/shard_map/ppermute | solution.py:162
